TPU v7x, 32 devices: a whole 2x2x4 slice. The times are simulated.
32 devices in a mesh: gx: 4 (over y, core), gy: 8 (over z, x).
Axes of the slice: x: 2, y: 2, z: 4, core: 2. Of those that a mesh axis runs over, the one named last changes fastest.
Arguments:
- outline: float32 [128, 512, 512], P('gx', 'gy'), may hold values from -0.7 to 0.7, as said below
- centres: float32 [128, 512, 2], P('gx', 'gy'), may hold values from -0.75 to 0.75
- velocity: float32 [128, 512, 2], P('gx', 'gy'), may hold values from -6 to 6
- mass: float32 [128, 512], P('gx', 'gy'), may hold values from 0.5 to 4
- response: float32 [128, 512, 64], P('gx', 'gy'), may hold values from -0.75 to 0.75
- pairs: int32 [4, 8, 512, 4], P('gx', 'gy'), may hold values from 0 to 2047, as said below
- pair_count: int32 [4, 8], P('gx', 'gy'), may hold values from 1 to 512, as said below
- forcing: float32 [65536, 128], P(('gx', 'gy')), may hold values from -6 to 6
- ocean_dest: int32 [65536, 1], P(('gx', 'gy')), may hold values from 0 to 31; in each aligned block of 2048 rows (0 to 2047, 2048 to 4095, ...) at most 160 rows name the same one
- ocean_floe: int32 [65536], P(('gx', 'gy')), may hold values from 0 to 2047
Outputs:
- final_velocity: float32 [128, 512, 2], P('gx', 'gy')
- final_centres: float32 [128, 512, 2], P('gx', 'gy')
Inputs may be any that keep to these rules, and one draw needn't show every extreme that they name: `pairs`: each slot holds a local floe below 2048, a neighbour code below 8, and two tiles below 2; slots from pair_count on are padding. `pair_count`: some block's list is full. `ocean_dest`: the rows of one block name any one block at most 160 times. `outline`: polygon vertices lie at radii 0.3 to 0.7 around the centre, in order of angle.
All inputs are finite; a program needn't handle non-finite values.
Results may differ from a plain program's by a relative error of at most 0.0003.
Values sent between devices are 32-bit elements; how exact they have to be, the bound alone decides.
A program may use at most 128 MiB of HBM per device.

v0:
```python
import math

import jax
import jax.numpy as jnp
from jax import lax
from jax.sharding import PartitionSpec as P

TILE = 128
STEPS = 3


DIRX = (-1, -1, -1, 0, 0, 1, 1, 1)
DIRY = (-1, 0, 1, -1, 1, -1, 0, 1)
KAPPA = 1.0
INV_WIDTH = 100.0
DT = 0.1
DRAG = 0.5


def with_halo(cells, sides, width):
    for axis, dim in sides:
        count = lax.axis_size(axis)
        ends = count - 1
        head = lax.slice_in_dim(cells, 0, width, axis=dim)
        tail = lax.slice_in_dim(cells, cells.shape[dim] - width, cells.shape[dim], axis=dim)
        cells = jnp.concatenate(
            [
                lax.ppermute(tail, axis, [(i, (i + 1) % count) for i in range(ends)]),
                cells,
                lax.ppermute(head, axis, [((i + 1) % count, i) for i in range(ends)]),
            ],
            axis=dim,
        )
    return cells


def tile_force(own, other, step_x, step_y):
    diff_x = own[:, 0, :, None] - other[:, 0, None, :] - step_x[:, None, None]
    diff_y = own[:, 1, :, None] - other[:, 1, None, :] - step_y[:, None, None]
    weight = jnp.exp(-(diff_x * diff_x + diff_y * diff_y) * INV_WIDTH)
    return KAPPA * jnp.stack(
        [jnp.sum(weight * diff_x, axis=(1, 2)), jnp.sum(weight * diff_y, axis=(1, 2))], axis=1
    )


def table_pick(code, table):
    match = code[:, None] == jnp.arange(8, dtype=jnp.int32)[None, :]
    return jnp.sum(jnp.where(match, jnp.asarray(table, dtype=jnp.int32)[None, :], 0), axis=1)


def tile_terms(rows_table, ntiles, own_idx, own_tile, other_idx, other_tile, step_x, step_y, valid):
    size_b = math.gcd(own_idx.shape[0], 256)
    own_key = own_idx * ntiles + own_tile
    other_key = other_idx * ntiles + other_tile

    def block(items):
        ok_own, ok_other, sx, sy, ok = items
        own = jnp.take(rows_table, ok_own, axis=0)
        other = jnp.take(rows_table, ok_other, axis=0)
        return (
            tile_force(own, other, sx.astype(jnp.float32), sy.astype(jnp.float32))
            * ok.astype(jnp.float32)[:, None]
        )

    def shaped(arr):
        return arr.reshape(-1, size_b)

    return lax.map(
        block, (shaped(own_key), shaped(other_key), shaped(step_x), shaped(step_y), shaped(valid))
    ).reshape(-1, 2)


def contact_forces(extended, pairs, pair_count):
    rows_x = extended.shape[0] - 2
    cols_y = extended.shape[1] - 2
    width = cols_y + 2
    nverts = extended.shape[2] // 2
    ntiles = nverts // TILE
    rows_table = jnp.transpose(extended.reshape(-1, 2, ntiles, TILE), (0, 2, 1, 3)).reshape(
        -1, 2, TILE
    )
    slots = pairs.shape[2]
    lists = pairs[0, 0]
    local = lists[:, 0]
    code = lists[:, 1]
    step_x = table_pick(code, DIRX)
    step_y = table_pick(code, DIRY)
    row = local // cols_y
    col = local % cols_y
    prow = row + step_x
    pcol = col + step_y
    glob_row = lax.axis_index("gx") * rows_x + prow
    glob_col = lax.axis_index("gy") * cols_y + pcol
    inside = (
        (glob_row >= 0)
        & (glob_row < rows_x * lax.axis_size("gx"))
        & (glob_col >= 0)
        & (glob_col < cols_y * lax.axis_size("gy"))
    )
    valid = (jnp.arange(slots, dtype=jnp.int32) < pair_count[0, 0]) & inside
    own_idx = (row + 1) * width + col + 1
    other_idx = (prow + 1) * width + pcol + 1
    forces = tile_terms(
        rows_table, ntiles, own_idx, lists[:, 2], other_idx, lists[:, 3], step_x, step_y, valid
    )
    accum = jnp.zeros(((rows_x + 2) * width, 2), jnp.float32)
    accum = accum.at[own_idx].add(forces).at[other_idx].add(-forces)
    accum = accum.reshape(rows_x + 2, width, 2)
    rim = with_halo(accum, (("gx", 0), ("gy", 1)), 1)
    total = rim[2 : rows_x + 2, 2 : cols_y + 2]
    total = total.at[0].add(rim[0, 2 : cols_y + 2])
    total = total.at[rows_x - 1].add(rim[rows_x + 3, 2 : cols_y + 2])
    total = total.at[:, 0].add(rim[2 : rows_x + 2, 0])
    total = total.at[:, cols_y - 1].add(rim[2 : rows_x + 2, cols_y + 3])
    total = total.at[0, 0].add(rim[0, 0])
    total = total.at[0, cols_y - 1].add(rim[0, cols_y + 3])
    total = total.at[rows_x - 1, 0].add(rim[rows_x + 3, 0])
    total = total.at[rows_x - 1, cols_y - 1].add(rim[rows_x + 3, cols_y + 3])
    return total


def shards(
    outline, centres, velocity, mass, response, pairs, pair_count, forcing, ocean_dest, ocean_floe
):
    rows_x, cols_y, span = outline.shape
    nverts = span // 2
    rows_dev, row_width = forcing.shape
    bins = row_width // 2
    devices = lax.axis_size(("gx", "gy"))
    capacity = max(2, 5 * rows_dev // (2 * devices))
    dest = ocean_dest[:, 0]
    onehot = (dest[:, None] == jnp.arange(devices, dtype=jnp.int32)[None, :]).astype(jnp.int32)
    slot = jnp.sum((jnp.cumsum(onehot, axis=0) - 1) * onehot, axis=1)
    place = dest * capacity + slot
    send_rows = jnp.zeros((devices * capacity, row_width), jnp.float32).at[place].set(forcing)
    send_floe = (
        jnp.zeros((devices * capacity,), jnp.float32).at[place].set(ocean_floe.astype(jnp.float32))
    )
    got_rows, got_floe = (
        lax.all_to_all(
            send_rows.reshape(devices, capacity, row_width),
            ("gx", "gy"),
            split_axis=0,
            concat_axis=0,
            tiled=True,
        ),
        lax.all_to_all(
            send_floe.reshape(devices, capacity),
            ("gx", "gy"),
            split_axis=0,
            concat_axis=0,
            tiled=True,
        ),
    )
    floe_index = got_floe.reshape(-1).astype(jnp.int32)
    ocean_sum = (
        jnp.zeros((rows_x * cols_y, row_width), jnp.float32)
        .at[floe_index]
        .add(got_rows.reshape(-1, row_width))
    )
    ocean_sum = ocean_sum.reshape(rows_x, cols_y, 2, bins)
    ocean_force = jnp.einsum("xycb,xyb->xyc", ocean_sum, response, precision=lax.Precision.HIGHEST)
    shift = centres
    vel = velocity
    for step in range(STEPS):
        positions = outline + jnp.repeat(shift, nverts, axis=2)
        extended = with_halo(positions, (("gx", 0), ("gy", 1)), 1)
        contact = contact_forces(extended, pairs, pair_count)
        vel = vel + DT * (contact + ocean_force - DRAG * vel) / mass[..., None]
        shift = shift + DT * vel
    return (vel, shift)


def solution(mesh):
    return jax.shard_map(
        shards,
        mesh=mesh,
        in_specs=(
            P("gx", "gy", None),
            P("gx", "gy", None),
            P("gx", "gy", None),
            P("gx", "gy"),
            P("gx", "gy", None),
            P("gx", "gy", None, None),
            P("gx", "gy"),
            P(("gx", "gy"), None),
            P(("gx", "gy"), None),
            P(("gx", "gy")),
        ),
        out_specs=(P("gx", "gy", None), P("gx", "gy", None)),
        check_vma=False,
    )
```

profile of v0, /device:TPU:3, one launch (start us, length us, event | category | flops | bytes accessed | tf_op | source)
XLA Modules:
  0.0 507.2 jit_solution(15284350786337915942)
XLA Ops:
  5.8 6.5 %reshape.1041 = f32[32,64,512]{2,1,0:T(8,128)} reshape(f32[32,64,2,256]{3,2,1,0:T(2,128)} %broadcast_in_dim.107) | data formatting | bytes 8388608 | tf_op jit(solution)/shard_map/reshape | solution.py:166
  24.5 9.1 %reduce-window.6 = s32[32,16,128]{2,1,0:T(8,128)S(1)} reduce-window(s32[32,16,128]{2,1,0:T(8,128)S(1)} %fusion.21, s32[]{:T(128)} %constant.685.clone.1), window={size=1x1x128 pad=0_0x0_0x127_0}, to_apply=%region_9.11 | reduce-window | flops 8323072 | bytes 524292 | tf_op jit(solution)/shard_map/reduce-window
  34.4 8.1 %scatter_custom_fusion.2 = f32[5120]{0:T(1024)S(1)} fusion(s32[2048]{0:T(1024)S(1)} %bitcast.266, f32[2048]{0:T(1024)S(1)} %convert_element_type.112, f32[]{:T(128)} %constant.683.clone.1), kind=kCustom, calls=%fused_computation.145 | custom fusion | bytes 20484 | tf_op jit(solution)/shard_map/scatter | solution.py:137
  51.3 7.5 %scatter_custom_fusion.3 = f32[5120,128]{1,0:T(8,128)} fusion(s32[2048]{0:T(1024)S(1)} %bitcast.267, f32[2048,128]{1,0:T(8,128)} %param.79, f32[]{:T(128)} %constant.683.clone.1), kind=kCustom, calls=%fused_computation.84 | custom fusion | bytes 2621952 | tf_op jit(solution)/shard_map/scatter | solution.py:135
  66.2 6.8 %all-to-all-start.1 = ((f32[32,160,128]{2,1,0:T(8,128)}), f32[32,160,128]{2,1,0:T(8,128)}, u32[]{:S(2)}, u32[]{:S(2)}) async-start(f32[32,160,128]{2,1,0:T(8,128)} %bitcast.206), calls=%async_computation.1 | async-start | bytes 5242880 | tf_op jit(solution)/shard_map/all_to_all | solution.py:140
  77.8 6.5 %reshape.1042 = f32[2244,2,2,128]{3,2,1,0:T(2,128)} reshape(f32[34,66,512]{2,1,0:T(8,128)} %pad_maximum_fusion) | data formatting | bytes 9191424 | tf_op jit(solution)/shard_map/reshape | solution.py:79
  88.1 15.2 %copy.432 = f32[4488,2,128]{2,1,0:T(2,128)} copy(f32[4488,2,128]{2,0,1:T(8,128)S(1)} %bitcast.200) | data formatting | bytes 9191424 | tf_op jit(solution)/shard_map/while | solution.py:68
  103.3 45.6 %while.54 = (s32[]{:T(128)}, f32[2,256,2]{1,2,0:T(2,128)S(1)}, s32[2,256]{1,0:T(2,128)S(1)}, f32[4488,2,128]{2,1,0:T(2,128)}, s32[2,256]{1,0:T(2,128)S(1)}, /*in...) while((s32[]{:T(128)}, f32[2,256,2]{1,2,0:T(2,128)S(1)}, ...), condition=%wide.region_5.7_spmd, body=%wide.region_2.6_spmd.sunk | while | flops 54664960 | bytes 3708269 | solution.py:68
  111.1 15.0 %multiply_reduce_fusion.9 = (f32[256]{0:T(256)S(1)}, f32[256]{0:T(256)S(1)}) fusion(f32[256]{0:T(256)S(1)} %bitcast.256, f32[256,128]{1,0:T(8,128)S(1)} %bitcast.208, f32[256,128]{1,0:T(8,128)S(1)} %bitcast.214, f32[256]{0:T(256)S(1)} %bitcast.255, f32[256,128]{1,0:T(8,128)S(1)} %bitcast.207, f32[256,128]{1,0:T(8,128)S(1)} %bitcast.213), kind=kLoop, calls=%fused_computation.16.clone.1 | loop fusion | flops 54525440 | bytes 528384 | tf_op jit(solution)/shard_map/while/body/eval_jaxpr/reduce_sum | solution.py:42
  134.0 15.0 %multiply_reduce_fusion.9 = (f32[256]{0:T(256)S(1)}, f32[256]{0:T(256)S(1)}) fusion(f32[256]{0:T(256)S(1)} %bitcast.256, f32[256,128]{1,0:T(8,128)S(1)} %bitcast.208, f32[256,128]{1,0:T(8,128)S(1)} %bitcast.214, f32[256]{0:T(256)S(1)} %bitcast.255, f32[256,128]{1,0:T(8,128)S(1)} %bitcast.207, f32[256,128]{1,0:T(8,128)S(1)} %bitcast.213), kind=kLoop, calls=%fused_computation.16.clone.1 | loop fusion | flops 54525440 | bytes 528384 | tf_op jit(solution)/shard_map/while/body/eval_jaxpr/reduce_sum | solution.py:42
  177.5 34.4 %scatter_custom_fusion.4 = f32[2048,128]{1,0:T(8,128)S(1)} fusion(s32[5120]{0:T(1024)S(1)} %bitcast.261, f32[5120,128]{1,0:T(8,128)} %bitcast.56, f32[]{:T(128)} %constant.683.clone.1), kind=kCustom, calls=%fused_computation.92 | custom fusion | flops 655360 | bytes 1049088 | tf_op jit(solution)/shard_map/scatter-add | solution.py:159
  214.5 15.3 %fusion.53 = f32[32,64,1,2]{3,2,1,0:T(1,128)S(1)} fusion(f32[32,64,2,64]{3,2,1,0:T(2,128)} %reshape.1051, f32[32,64,64,1]{2,3,1,0:T(1,128)S(1)} %bitcast.199), kind=kOutput, calls=%fused_computation.201 | convolution fusion | flops 3145728 | bytes 1589248 | tf_op jit(solution)/shard_map/xycb,xyb->xyc/dot_general | solution.py:162
  234.8 6.5 %reshape.1052 = f32[32,64,512]{2,1,0:T(8,128)} reshape(f32[32,64,2,256]{3,2,1,0:T(2,128)} %broadcast_in_dim.114) | data formatting | bytes 8388608 | tf_op jit(solution)/shard_map/reshape | solution.py:166
  268.3 6.5 %reshape.1053 = f32[2244,2,2,128]{3,2,1,0:T(2,128)} reshape(f32[34,66,512]{2,1,0:T(8,128)} %pad_maximum_fusion.1) | data formatting | bytes 9191424 | tf_op jit(solution)/shard_map/reshape | solution.py:79
  278.6 15.2 %copy.449 = f32[4488,2,128]{2,1,0:T(2,128)} copy(f32[4488,2,128]{2,0,1:T(8,128)S(1)} %bitcast.201) | data formatting | bytes 9191424 | tf_op jit(solution)/shard_map/while | solution.py:68
  293.8 45.6 %while.55 = (s32[]{:T(128)}, f32[2,256,2]{1,2,0:T(2,128)S(1)}, s32[2,256]{1,0:T(2,128)S(1)}, f32[4488,2,128]{2,1,0:T(2,128)}, s32[2,256]{1,0:T(2,128)S(1)}, /*in...) while((s32[]{:T(128)}, f32[2,256,2]{1,2,0:T(2,128)S(1)}, ...), condition=%wide.region_20.22_spmd, body=%wide.region_17.21_spmd.sunk | while | flops 54664960 | bytes 3708269 | solution.py:68
  301.6 15.0 %multiply_reduce_fusion.10 = (f32[256]{0:T(256)S(1)}, f32[256]{0:T(256)S(1)}) fusion(f32[256]{0:T(256)S(1)} %bitcast.258, f32[256,128]{1,0:T(8,128)S(1)} %bitcast.210, f32[256,128]{1,0:T(8,128)S(1)} %bitcast.216, f32[256]{0:T(256)S(1)} %bitcast.257, f32[256,128]{1,0:T(8,128)S(1)} %bitcast.209, f32[256,128]{1,0:T(8,128)S(1)} %bitcast.215), kind=kLoop, calls=%fused_computation.38.clone.1 | loop fusion | flops 54525440 | bytes 528384 | tf_op jit(solution)/shard_map/while/body/eval_jaxpr/reduce_sum | solution.py:42
  324.4 15.0 %multiply_reduce_fusion.10 = (f32[256]{0:T(256)S(1)}, f32[256]{0:T(256)S(1)}) fusion(f32[256]{0:T(256)S(1)} %bitcast.258, f32[256,128]{1,0:T(8,128)S(1)} %bitcast.210, f32[256,128]{1,0:T(8,128)S(1)} %bitcast.216, f32[256]{0:T(256)S(1)} %bitcast.257, f32[256,128]{1,0:T(8,128)S(1)} %bitcast.209, f32[256,128]{1,0:T(8,128)S(1)} %bitcast.215), kind=kLoop, calls=%fused_computation.38.clone.1 | loop fusion | flops 54525440 | bytes 528384 | tf_op jit(solution)/shard_map/while/body/eval_jaxpr/reduce_sum | solution.py:42
  372.4 6.5 %reshape.1057 = f32[32,64,512]{2,1,0:T(8,128)} reshape(f32[32,64,2,256]{3,2,1,0:T(2,128)} %broadcast_in_dim.117) | data formatting | bytes 8388608 | tf_op jit(solution)/shard_map/reshape | solution.py:166
  405.7 6.5 %reshape.1058 = f32[2244,2,2,128]{3,2,1,0:T(2,128)} reshape(f32[34,66,512]{2,1,0:T(8,128)} %pad_maximum_fusion.2) | data formatting | bytes 9191424 | tf_op jit(solution)/shard_map/reshape | solution.py:79
  416.0 15.2 %copy.461 = f32[4488,2,128]{2,1,0:T(2,128)} copy(f32[4488,2,128]{2,0,1:T(8,128)S(1)} %bitcast.202) | data formatting | bytes 9191424 | tf_op jit(solution)/shard_map/while | solution.py:68
  431.2 45.6 %while.56 = (s32[]{:T(128)}, f32[2,256,2]{1,2,0:T(2,128)S(1)}, s32[2,256]{1,0:T(2,128)S(1)}, f32[4488,2,128]{2,1,0:T(2,128)}, s32[2,256]{1,0:T(2,128)S(1)}, /*in...) while((s32[]{:T(128)}, f32[2,256,2]{1,2,0:T(2,128)S(1)}, ...), condition=%wide.region_28.30_spmd, body=%wide.region_25.29_spmd.sunk | while | flops 54664960 | bytes 3708269 | solution.py:68
  439.0 15.0 %multiply_reduce_fusion.11 = (f32[256]{0:T(256)S(1)}, f32[256]{0:T(256)S(1)}) fusion(f32[256]{0:T(256)S(1)} %bitcast.260, f32[256,128]{1,0:T(8,128)S(1)} %bitcast.212, f32[256,128]{1,0:T(8,128)S(1)} %bitcast.218, f32[256]{0:T(256)S(1)} %bitcast.259, f32[256,128]{1,0:T(8,128)S(1)} %bitcast.211, f32[256,128]{1,0:T(8,128)S(1)} %bitcast.217), kind=kLoop, calls=%fused_computation.60.clone.1 | loop fusion | flops 54525440 | bytes 528384 | tf_op jit(solution)/shard_map/while/body/eval_jaxpr/reduce_sum | solution.py:42
  461.9 15.0 %multiply_reduce_fusion.11 = (f32[256]{0:T(256)S(1)}, f32[256]{0:T(256)S(1)}) fusion(f32[256]{0:T(256)S(1)} %bitcast.260, f32[256,128]{1,0:T(8,128)S(1)} %bitcast.212, f32[256,128]{1,0:T(8,128)S(1)} %bitcast.218, f32[256]{0:T(256)S(1)} %bitcast.259, f32[256,128]{1,0:T(8,128)S(1)} %bitcast.211, f32[256,128]{1,0:T(8,128)S(1)} %bitcast.217), kind=kLoop, calls=%fused_computation.60.clone.1 | loop fusion | flops 54525440 | bytes 528384 | tf_op jit(solution)/shard_map/while/body/eval_jaxpr/reduce_sum | solution.py:42
  (325 shorter events, 248.3 us)
Async XLA Ops:
  18.8 40.8 %collective-permute-start = (f32[1,64,512]{2,1,0:T(8,128)S(1)}, f32[1,64,512]{2,1,0:T(8,128)S(1)}, u32[]{:S(2)}, u32[]{:S(2)}) collective-permute-start(f32[1,64,512]{2,1,0:T(8,128)S(1)} %get-tuple-element.632), channel_id=1, source_target_pairs={{0,8},{8,16},{16,24},{1,9},{9,17},{17,25},{2,10},{10,18},{18,26},{... | collective-permute-start | bytes 393224 | tf_op jit(solution)/shard_map/ppermute | solution.py:28
  22.5 37.1 %collective-permute-start.1 = (f32[1,64,512]{2,1,0:T(8,128)S(1)}, f32[1,64,512]{2,1,0:T(8,128)S(1)}, u32[]{:S(2)}, u32[]{:S(2)}) collective-permute-start(f32[1,64,512]{2,1,0:T(8,128)S(1)} %get-tuple-element.633), channel_id=1, source_target_pairs={{8,0},{16,8},{24,16},{9,1},{17,9},{25,17},{10,2},{18,10},{26,18},{... | collective-permute-start | bytes 393224 | tf_op jit(solution)/shard_map/ppermute | solution.py:30
  43.2 23.0 %all-to-all-start = ((f32[32,1,160]{2,1,0:T(1,128)}), f32[32,1,160]{2,1,0:T(1,128)S(1)}, u32[]{:S(2)}, u32[]{:S(2)}) async-start(f32[32,1,160]{2,1,0:T(1,128)} %all_to_all.9), calls=%async_computation | async-start | bytes 65536 | tf_op jit(solution)/shard_map/all_to_all | solution.py:147
  60.9 12.4 %collective-permute-start.2 = (f32[34,1,512]{2,0,1:T(8,128)S(1)}, f32[34,1,512]{2,0,1:T(8,128)S(1)}, u32[]{:S(2)}, u32[]{:S(2)}) collective-permute-start(f32[34,1,512]{2,0,1:T(8,128)S(1)} %copy.427), channel_id=1, source_target_pairs={{0,1},{1,2},{2,3},{3,4},{4,5},{5,6},{6,7},{8,9},{9,10},{10,11},{11... | collective-permute-start | bytes 208904 | tf_op jit(solution)/shard_map/ppermute | solution.py:28
  64.0 9.4 %collective-permute-start.3 = (f32[34,1,512]{2,0,1:T(8,128)S(1)}, f32[34,1,512]{2,0,1:T(8,128)S(1)}, u32[]{:S(2)}, u32[]{:S(2)}) collective-permute-start(f32[34,1,512]{2,0,1:T(8,128)S(1)} %copy.428), channel_id=1, source_target_pairs={{1,0},{2,1},{3,2},{4,3},{5,4},{6,5},{7,6},{9,8},{10,9},{11,10},{12... | collective-permute-start | bytes 208904 | tf_op jit(solution)/shard_map/ppermute | solution.py:30
  66.2 111.3 %all-to-all-start.1 = ((f32[32,160,128]{2,1,0:T(8,128)}), f32[32,160,128]{2,1,0:T(8,128)}, u32[]{:S(2)}, u32[]{:S(2)}) async-start(f32[32,160,128]{2,1,0:T(8,128)} %bitcast.206), calls=%async_computation.1 | async-start | bytes 5242880 | tf_op jit(solution)/shard_map/all_to_all | solution.py:140
  156.2 5.5 %collective-permute-start.4 = (f32[1,66,2]{1,0,2:T(1,128)S(1)}, f32[1,66,2]{1,0,2:T(1,128)S(1)}, u32[]{:S(2)}, u32[]{:S(2)}) collective-permute-start(f32[1,66,2]{1,0,2:T(1,128)S(1)} %bitcast.275), channel_id=1, source_target_pairs={{0,8},{8,16},{16,24},{1,9},{9,17},{17,25},{2,10},{10,18},{18,26},{... | collective-permute-start | bytes 1592 | tf_op jit(solution)/shard_map/ppermute | solution.py:28
  159.5 4.9 collective-permute-start.5
  164.5 5.5 %collective-permute-start.6 = (f32[36,1,2]{1,0,2:T(8,128)S(1)}, f32[36,1,2]{1,0,2:T(8,128)S(1)}, u32[]{:S(2)}, u32[]{:S(2)}) collective-permute-start(f32[36,1,2]{1,0,2:T(8,128)S(1)} %get-tuple-element.639), channel_id=1, source_target_pairs={{0,1},{1,2},{2,3},{3,4},{4,5},{5,6},{6,7},{8,9},{9,10},{10,11},{11... | collective-permute-start | bytes 872 | tf_op jit(solution)/shard_map/ppermute | solution.py:28
  167.6 5.6 %collective-permute-start.7 = (f32[36,1,2]{1,0,2:T(8,128)S(1)}, f32[36,1,2]{1,0,2:T(8,128)S(1)}, u32[]{:S(2)}, u32[]{:S(2)}) collective-permute-start(f32[36,1,2]{1,0,2:T(8,128)S(1)} %get-tuple-element.638), channel_id=1, source_target_pairs={{1,0},{2,1},{3,2},{4,3},{5,4},{6,5},{7,6},{9,8},{10,9},{11,10},{12... | collective-permute-start | bytes 872 | tf_op jit(solution)/shard_map/ppermute | solution.py:30
  247.7 6.3 %collective-permute-start.9 = (f32[1,64,512]{2,1,0:T(8,128)S(1)}, f32[1,64,512]{2,1,0:T(8,128)S(1)}, u32[]{:S(2)}, u32[]{:S(2)}) collective-permute-start(f32[1,64,512]{2,1,0:T(8,128)S(1)} %get-tuple-element.631), channel_id=1, source_target_pairs={{8,0},{16,8},{24,16},{9,1},{17,9},{25,17},{10,2},{18,10},{26,18},{... | collective-permute-start | bytes 393224 | tf_op jit(solution)/shard_map/ppermute | solution.py:30
  254.1 5.7 %collective-permute-start.10 = (f32[34,1,512]{2,0,1:T(8,128)S(1)}, f32[34,1,512]{2,0,1:T(8,128)S(1)}, u32[]{:S(2)}, u32[]{:S(2)}) collective-permute-start(f32[34,1,512]{2,0,1:T(8,128)S(1)} %copy.444), channel_id=1, source_target_pairs={{0,1},{1,2},{2,3},{3,4},{4,5},{5,6},{6,7},{8,9},{9,10},{10,11},{11... | collective-permute-start | bytes 208904 | tf_op jit(solution)/shard_map/ppermute | solution.py:28
  257.8 6.1 %collective-permute-start.11 = (f32[34,1,512]{2,0,1:T(8,128)S(1)}, f32[34,1,512]{2,0,1:T(8,128)S(1)}, u32[]{:S(2)}, u32[]{:S(2)}) collective-permute-start(f32[34,1,512]{2,0,1:T(8,128)S(1)} %copy.445), channel_id=1, source_target_pairs={{1,0},{2,1},{3,2},{4,3},{5,4},{6,5},{7,6},{9,8},{10,9},{11,10},{12... | collective-permute-start | bytes 208904 | tf_op jit(solution)/shard_map/ppermute | solution.py:30
  346.4 5.3 %collective-permute-start.12 = (f32[1,66,2]{1,0,2:T(1,128)S(1)}, f32[1,66,2]{1,0,2:T(1,128)S(1)}, u32[]{:S(2)}, u32[]{:S(2)}) collective-permute-start(f32[1,66,2]{1,0,2:T(1,128)S(1)} %bitcast.276), channel_id=1, source_target_pairs={{0,8},{8,16},{16,24},{1,9},{9,17},{17,25},{2,10},{10,18},{18,26},{... | collective-permute-start | bytes 1592 | tf_op jit(solution)/shard_map/ppermute | solution.py:28
  349.6 4.9 collective-permute-start.13
  354.6 5.5 %collective-permute-start.14 = (f32[36,1,2]{1,0,2:T(8,128)S(1)}, f32[36,1,2]{1,0,2:T(8,128)S(1)}, u32[]{:S(2)}, u32[]{:S(2)}) collective-permute-start(f32[36,1,2]{1,0,2:T(8,128)S(1)} %get-tuple-element.637), channel_id=1, source_target_pairs={{0,1},{1,2},{2,3},{3,4},{4,5},{5,6},{6,7},{8,9},{9,10},{10,11},{11... | collective-permute-start | bytes 872 | tf_op jit(solution)/shard_map/ppermute | solution.py:28
  358.1 5.6 %collective-permute-start.15 = (f32[36,1,2]{1,0,2:T(8,128)S(1)}, f32[36,1,2]{1,0,2:T(8,128)S(1)}, u32[]{:S(2)}, u32[]{:S(2)}) collective-permute-start(f32[36,1,2]{1,0,2:T(8,128)S(1)} %get-tuple-element.636), channel_id=1, source_target_pairs={{1,0},{2,1},{3,2},{4,3},{5,4},{6,5},{7,6},{9,8},{10,9},{11,10},{12... | collective-permute-start | bytes 872 | tf_op jit(solution)/shard_map/ppermute | solution.py:30
  383.4 5.3 %collective-permute-start.16 = (f32[1,64,512]{2,1,0:T(8,128)S(1)}, f32[1,64,512]{2,1,0:T(8,128)S(1)}, u32[]{:S(2)}, u32[]{:S(2)}) collective-permute-start(f32[1,64,512]{2,1,0:T(8,128)S(1)} %get-tuple-element.628), channel_id=1, source_target_pairs={{0,8},{8,16},{16,24},{1,9},{9,17},{17,25},{2,10},{10,18},{18,26},{... | collective-permute-start | bytes 393224 | tf_op jit(solution)/shard_map/ppermute | solution.py:28
  386.7 6.3 %collective-permute-start.17 = (f32[1,64,512]{2,1,0:T(8,128)S(1)}, f32[1,64,512]{2,1,0:T(8,128)S(1)}, u32[]{:S(2)}, u32[]{:S(2)}) collective-permute-start(f32[1,64,512]{2,1,0:T(8,128)S(1)} %get-tuple-element.629), channel_id=1, source_target_pairs={{8,0},{16,8},{24,16},{9,1},{17,9},{25,17},{10,2},{18,10},{26,18},{... | collective-permute-start | bytes 393224 | tf_op jit(solution)/shard_map/ppermute | solution.py:30
  393.2 6.1 %collective-permute-start.18 = (f32[34,1,512]{2,0,1:T(8,128)S(1)}, f32[34,1,512]{2,0,1:T(8,128)S(1)}, u32[]{:S(2)}, u32[]{:S(2)}) collective-permute-start(f32[34,1,512]{2,0,1:T(8,128)S(1)} %copy.456), channel_id=1, source_target_pairs={{0,1},{1,2},{2,3},{3,4},{4,5},{5,6},{6,7},{8,9},{9,10},{10,11},{11... | collective-permute-start | bytes 208904 | tf_op jit(solution)/shard_map/ppermute | solution.py:28
  395.1 6.2 %collective-permute-start.19 = (f32[34,1,512]{2,0,1:T(8,128)S(1)}, f32[34,1,512]{2,0,1:T(8,128)S(1)}, u32[]{:S(2)}, u32[]{:S(2)}) collective-permute-start(f32[34,1,512]{2,0,1:T(8,128)S(1)} %copy.457), channel_id=1, source_target_pairs={{1,0},{2,1},{3,2},{4,3},{5,4},{6,5},{7,6},{9,8},{10,9},{11,10},{12... | collective-permute-start | bytes 208904 | tf_op jit(solution)/shard_map/ppermute | solution.py:30
  483.8 5.1 collective-permute-start.20
  491.7 5.8 %collective-permute-start.22 = (f32[36,1,2]{1,0,2:T(8,128)S(1)}, f32[36,1,2]{1,0,2:T(8,128)S(1)}, u32[]{:S(2)}, u32[]{:S(2)}) collective-permute-start(f32[36,1,2]{1,0,2:T(8,128)S(1)} %get-tuple-element.635), channel_id=1, source_target_pairs={{0,1},{1,2},{2,3},{3,4},{4,5},{5,6},{6,7},{8,9},{9,10},{10,11},{11... | collective-permute-start | bytes 872 | tf_op jit(solution)/shard_map/ppermute | solution.py:28
  495.6 5.6 %collective-permute-start.23 = (f32[36,1,2]{1,0,2:T(8,128)S(1)}, f32[36,1,2]{1,0,2:T(8,128)S(1)}, u32[]{:S(2)}, u32[]{:S(2)}) collective-permute-start(f32[36,1,2]{1,0,2:T(8,128)S(1)} %get-tuple-element.634), channel_id=1, source_target_pairs={{1,0},{2,1},{3,2},{4,3},{5,4},{6,5},{7,6},{9,8},{10,9},{11,10},{12... | collective-permute-start | bytes 872 | tf_op jit(solution)/shard_map/ppermute | solution.py:30
  (16 other events, 507.8 us)
where the time goes:
time: 515 us; the launch traced here: 507 us
  other arithmetic  193 us (37%)
  local copies, waits for them, and re-layouts  186 us (36%)
  starting transfers between devices  76.3 us (15%)
  waiting for transfers between devices  33.2 us (6%)
  matrix products  15.3 us (3%)
    reduce_sum x6, other arithmetic, tile_force(): jnp.sum(weight * diff_x, axis=(1, 2))  89.8 us
    while x3, local copies, waits for them, and re-layouts, tile_terms(): lax.map(block, (shaped(own_key), shaped(other_key), shaped(step_x), shape...  45.6 us
    ppermute x12, starting transfers between devices, with_halo(): lax.ppermute(tail, axis, [(i, (i + 1) % count) for i in range(ends)])  37.2 us
    scatter-add x1, other arithmetic, shards(): ocean_sum = jnp.zeros((rows_x * cols_y, row_width), jnp.float32).at[floe_...  34.4 us
    ppermute x12, waiting for transfers between devices, with_halo(): lax.ppermute(head, axis, [((i + 1) % count, i) for i in range(ends)])  32.6 us
    ppermute x12, starting transfers between devices, with_halo(): lax.ppermute(head, axis, [((i + 1) % count, i) for i in range(ends)])  25.9 us
    gather x6, local copies, waits for them, and re-layouts, block(): own = jnp.take(rows_table, ok_own, axis=0)  19.8 us
    gather x6, local copies, waits for them, and re-layouts, block(): other = jnp.take(rows_table, ok_other, axis=0)  19.8 us
  transfers between devices with their start and end apart: 26, of which 11 were waited for; matrix products, arithmetic and copies ran while one was open for 23% of the time, Pallas kernels for 0%

commit v1 on v0

v1 whole, which is shorter than its diff:
```python
import functools
import math

import jax
import jax.numpy as jnp
from jax import lax
from jax.experimental import pallas as pl
from jax.experimental.pallas import tpu as pltpu
from jax.sharding import PartitionSpec as P

MESH = pl.DeviceIdType.MESH
TILE = 128
STEPS = 3

DIRX = (-1, -1, -1, 0, 0, 1, 1, 1)
DIRY = (-1, 0, 1, -1, 1, -1, 0, 1)
INV_WIDTH = 100.0
DT = 0.1
DRAG = 0.5
SCALE = math.sqrt(INV_WIDTH * math.log2(math.e))
NT = (((1,), (1,)), ((), ()))
EXACT = lax.Precision.HIGHEST
VMEM_BYTES = 48 * 1024 * 1024


def up_to(value, step):
    return -(-value // step) * step


def split_two(value):
    high = value.astype(jnp.bfloat16)
    low = (value - high.astype(jnp.float32)).astype(jnp.bfloat16)
    return jnp.concatenate([high, low], axis=1)


def hot(match):
    return jnp.where(match, 1.0, 0.0).astype(jnp.bfloat16)


def in_vmem():
    return pl.BlockSpec(memory_space=pltpu.VMEM)


def pack_kernel(devices, cap, cols, dest_ref, floe_ref, rows_ref, out_ref, place, halves, names):
    count = dest_ref.shape[1]
    width = 256
    before = hot(
        lax.broadcasted_iota(jnp.int32, (width, width), 0)
        < lax.broadcasted_iota(jnp.int32, (width, width), 1)
    )
    owner = lax.broadcasted_iota(jnp.int32, (devices, width), 0)
    offset = jnp.zeros((devices, 1), jnp.float32)
    for start in range(0, count, width):
        dest = dest_ref[:, start : start + width]
        match = owner == dest
        earlier = jnp.dot(hot(match), before, preferred_element_type=jnp.float32) + offset
        slot = jnp.sum(jnp.where(match, earlier, 0.0), axis=0, keepdims=True)
        place[:, start : start + width] = dest * cap + slot.astype(jnp.int32)
        offset = offset + jnp.sum(jnp.where(match, 1.0, 0.0), axis=1, keepdims=True)
    halves[...] = split_two(rows_ref[...])
    floe = floe_ref[...]
    names[...] = jnp.concatenate(
        [(floe // cols).astype(jnp.float32), (floe % cols).astype(jnp.float32)]
        + [jnp.zeros((1, count), jnp.float32)] * 14,
        axis=0,
    ).astype(jnp.bfloat16)

    def one(device, carry):
        slots = lax.broadcasted_iota(jnp.int32, (cap, count), 0) + device * cap
        chosen = hot(slots == place[...])
        both = jnp.dot(chosen, halves[...], preferred_element_type=jnp.float32)
        out_ref[device, 0:cap, :] = both[:, :128] + both[:, 128:]
        name = lax.dot_general(names[...], chosen, NT, preferred_element_type=jnp.float32)
        local = name[0:1] * float(cols) + name[1:2]
        out_ref[device, cap : cap + 8, :] = jnp.zeros((8, 128), jnp.float32)
        for start in range(0, cap, 128):
            size = min(128, cap - start)
            line = cap + start // 128
            out_ref[device, line : line + 1, 0:size] = local[:, start : start + size]
        return carry

    lax.fori_loop(0, devices, one, 0)


def ocean_kernel(devices, cap, index_ref, rows_ref, response_ref, out_ref, halves):
    total = devices * cap
    block = 256

    def split(device, carry):
        start = pl.multiple_of(device * cap, 16)
        halves[pl.ds(start, cap), :] = split_two(rows_ref[device, 0:cap, :])
        return carry

    lax.fori_loop(0, devices, split, 0)
    lane = lax.broadcasted_iota(jnp.int32, (8, 128), 1)
    line = lax.broadcasted_iota(jnp.int32, (8, 128), 0)
    ends = jnp.where(lane // 64 == line, 1.0, 0.0)

    def one(step, carry):
        start = pl.multiple_of(step * block, block)
        floes = lax.broadcasted_iota(jnp.int32, (block, total), 0) + start
        chosen = hot(floes == index_ref[...])
        both = jnp.dot(chosen, halves[...], preferred_element_type=jnp.float32)
        reply = response_ref[pl.ds(start, block), :]
        product = (both[:, :128] + both[:, 128:]) * jnp.concatenate([reply, reply], axis=1)
        out_ref[:, pl.ds(start, block)] = lax.dot_general(
            ends, product, NT, precision=EXACT, preferred_element_type=jnp.float32
        )
        return carry

    lax.fori_loop(0, out_ref.shape[1] // block, one, 0)


def gather_kernel(index_ref, outline_ref, rim_ref, ox_ref, oy_ref, px_ref, py_ref, table, ox, oy, px, py, sems):
    floes = outline_ref.shape[0]
    inner = pltpu.make_async_copy(outline_ref, table.at[pl.ds(0, floes)], sems.at[0])
    outer = pltpu.make_async_copy(rim_ref, table.at[pl.ds(floes, rim_ref.shape[0])], sems.at[1])
    inner.start()
    outer.start()
    inner.wait()
    outer.wait()
    slots = ox.shape[0]
    half = 2 * TILE

    def one(group, carry):
        for part in range(8):
            slot = group * 8 + part
            own = table[pl.ds(index_ref[0, slot], 1), :]
            own_first = index_ref[1, slot] == 0
            other = table[pl.ds(index_ref[2, slot], 1), :]
            other_first = index_ref[3, slot] == 0
            at = pl.ds(slot, 1)
            ox[at, :] = jnp.where(own_first, own[:, :TILE], own[:, TILE:half])
            oy[at, :] = jnp.where(own_first, own[:, half : half + TILE], own[:, half + TILE :])
            px[at, :] = jnp.where(other_first, other[:, :TILE], other[:, TILE:half])
            py[at, :] = jnp.where(other_first, other[:, half : half + TILE], other[:, half + TILE :])
        return carry

    lax.fori_loop(0, slots // 8, one, 0)
    for source, out in ((ox, ox_ref), (oy, oy_ref), (px, px_ref), (py, py_ref)):
        for start in range(0, slots, 128):
            out[:, start : start + 128] = source[start : start + 128, :].T


def steps_kernel(
    nx, ny, rows, cols, ox_ref, oy_ref, px_ref, py_ref, meta_ref, state_ref, out_ref,
    px2, py2, pq, ax_ref, ay_ref, own_row, own_col, force, state, total, sums,
    first_line, first_side, later_line, later_side, send_sem, recv_sem,
):
    my_x = lax.axis_index("gx")
    my_y = lax.axis_index("gy")
    slots = ox_ref.shape[1]
    high = state_ref.shape[1]

    def present(dx, dy):
        x, y = my_x + dx, my_y + dy
        return (x >= 0) & (x < nx) & (y >= 0) & (y < ny)

    barrier = pltpu.get_barrier_semaphore()
    for dx, dy in zip(DIRX, DIRY):
        @pl.when(present(dx, dy))
        def _():
            pl.semaphore_signal(
                barrier, inc=1, device_id=(my_x + dx, my_y + dy), device_id_type=MESH
            )
    wide = jnp.where(my_x > 0, 2, 1) + jnp.where(my_x < nx - 1, 1, 0)
    deep = jnp.where(my_y > 0, 2, 1) + jnp.where(my_y < ny - 1, 1, 0)
    pl.semaphore_wait(barrier, wide * deep - 1)

    def descriptor(turn, way, source, sign):
        dx, dy = DIRX[way], DIRY[way]
        if dx == 0:
            landing = first_side if turn == 0 else later_side.at[turn - 1]
            landing = landing.at[(dy + 1) // 2]
            part = source
        else:
            landing = first_line if turn == 0 else later_line.at[turn - 1]
            landing = landing.at[way if way < 3 else way - 2]
            part = source.at[:, pl.ds(0 if dx < 0 else rows, 8), :]
        return pltpu.make_async_remote_copy(
            src_ref=part,
            dst_ref=landing,
            send_sem=send_sem.at[turn, way],
            recv_sem=recv_sem.at[turn, way],
            device_id=(my_x + sign * dx, my_y + sign * dy),
            device_id_type=MESH,
        )

    def send(turn, source):
        for way in range(8):
            @pl.when(present(DIRX[way], DIRY[way]))
            def _():
                descriptor(turn, way, source, 1).start()

    def collect(turn, source, into):
        number = into.shape[0]
        for way in range(8):
            dx, dy = DIRX[way], DIRY[way]

            @pl.when(present(-dx, -dy))
            def _():
                descriptor(turn, way, source, -1).wait_recv()
                if dx == 0:
                    landing = first_side if turn == 0 else later_side.at[turn - 1]
                    landing = landing.at[(dy + 1) // 2]
                    top, size = 0, high
                else:
                    landing = first_line if turn == 0 else later_line.at[turn - 1]
                    landing = landing.at[way if way < 3 else way - 2]
                    top, size = (rows if dx < 0 else 0), 8
                lane = lax.broadcasted_iota(jnp.int32, (size, 128), 1)
                line = lax.broadcasted_iota(jnp.int32, (size, 128), 0)
                keep = lane >= 0
                if dx != 0:
                    keep = keep & (line < 2)
                if dy != 0:
                    left = cols if dy < 0 else 0
                    keep = keep & (lane >= left) & (lane < left + 2)
                for part in range(number):
                    piece = landing[part]
                    if dy != 0:
                        piece = pltpu.roll(piece, (cols if dy < 0 else 128 - cols), 1)
                    into[part, top : top + size, :] += jnp.where(keep, piece, 0.0)

    send(0, state_ref)
    state[...] = state_ref[...]

    px = px_ref[...] * SCALE
    py = py_ref[...] * SCALE
    px2[...] = 2.0 * px
    py2[...] = 2.0 * py
    pq[...] = -(px * px + py * py)
    meta = meta_ref[...]
    line_of = jnp.concatenate([meta[0:1], meta[2:3]], axis=1)
    lane_of = jnp.concatenate([meta[1:2], meta[3:4]], axis=1)
    own_row[...] = jnp.where(
        lax.broadcasted_iota(jnp.int32, (high, 2 * slots), 0) == line_of, 1.0, 0.0
    )
    own_col[...] = jnp.where(
        lax.broadcasted_iota(jnp.int32, (128, 2 * slots), 0) == lane_of, 1.0, 0.0
    )
    valid = meta[4:5] > 0
    step_x = meta[5:6].astype(jnp.float32)
    step_y = meta[6:7].astype(jnp.float32)
    collect(0, state_ref, state)
    mass = jnp.where(state[4] == 0.0, 1.0, state[4])

    tall = 64

    for step in range(STEPS):
        shift = jnp.concatenate([state[0], state[1]], axis=0)
        picked = jnp.dot(shift, own_col[...], precision=EXACT, preferred_element_type=jnp.float32)
        at_x = jnp.sum(picked[:high] * own_row[...], axis=0, keepdims=True)
        at_y = jnp.sum(picked[high:] * own_row[...], axis=0, keepdims=True)
        gap_x = at_x[:, :slots] - at_x[:, slots:] - step_x
        gap_y = at_y[:, :slots] - at_y[:, slots:] - step_y
        ax_ref[...] = (ox_ref[...] + gap_x) * SCALE
        ay_ref[...] = (oy_ref[...] + gap_y) * SCALE

        def block(number, carry):
            at = pl.ds(pl.multiple_of(number * 128, 128), 128)
            zero = jnp.zeros((8, 128), jnp.float32)
            along_x, along_y, back_x, back_y = zero, zero, zero, zero
            for start in range(0, TILE, tall):
                ax = ax_ref[start : start + tall, at]
                ay = ay_ref[start : start + tall, at]
                aq = -(ax * ax + ay * ay)

                def vertex(group, sums_now):
                    over_w, bx, by = sums_now
                    base = pl.multiple_of(group * 8, 8)
                    qx = px2[pl.ds(base, 8), at]
                    qy = py2[pl.ds(base, 8), at]
                    qq = pq[pl.ds(base, 8), at]
                    for w in range(8):
                        rx, ry, rq = qx[w : w + 1], qy[w : w + 1], qq[w : w + 1]
                        weight = jnp.exp2((ax * rx + aq) + (ay * ry + rq))
                        over_w = over_w + weight
                        over_u = jnp.sum(weight.reshape(tall // 8, 8, 128), axis=0)
                        bx = bx + over_u * rx
                        by = by + over_u * ry
                    return over_w, bx, by

                over_w, back_x, back_y = lax.fori_loop(
                    0, TILE // 8, vertex,
                    (jnp.zeros((tall, 128), jnp.float32), back_x, back_y),
                )
                along_x = along_x + jnp.sum((ax * over_w).reshape(tall // 8, 8, 128), axis=0)
                along_y = along_y + jnp.sum((ay * over_w).reshape(tall // 8, 8, 128), axis=0)
            force[0:1, at] = jnp.sum(along_x - 0.5 * back_x, axis=0, keepdims=True) / SCALE
            force[1:2, at] = jnp.sum(along_y - 0.5 * back_y, axis=0, keepdims=True) / SCALE
            return carry

        lax.fori_loop(0, slots // 128, block, 0)
        force_x = jnp.where(valid, force[0:1, :], 0.0)
        force_y = jnp.where(valid, force[1:2, :], 0.0)
        both_x = jnp.concatenate([force_x, -force_x], axis=1)
        both_y = jnp.concatenate([force_y, -force_y], axis=1)
        spread = jnp.concatenate([own_row[...] * both_x, own_row[...] * both_y], axis=0)
        placed = lax.dot_general(
            spread, own_col[...], NT, precision=EXACT, preferred_element_type=jnp.float32
        )
        mine = sums.at[step]
        mine[0] = placed[:high]
        mine[1] = placed[high:]
        send(step + 1, mine)
        total[0] = placed[:high]
        total[1] = placed[high:]
        collect(step + 1, mine, total)
        for axis in range(2):
            vel = state[2 + axis]
            vel = vel + DT * ((total[axis] + state[5 + axis]) - DRAG * vel) / mass
            state[2 + axis] = vel
            state[axis] = state[axis] + DT * vel

    out_ref[...] = state[0:4]
    for turn in range(STEPS + 1):
        for way in range(8):
            @pl.when(present(DIRX[way], DIRY[way]))
            def _():
                source = state_ref if turn == 0 else sums.at[turn - 1]
                descriptor(turn, way, source, 1).wait_send()


def table_pick(code, table):
    match = code[:, None] == jnp.arange(8, dtype=jnp.int32)[None, :]
    return jnp.sum(jnp.where(match, jnp.asarray(table, dtype=jnp.int32)[None, :], 0), axis=1)


def neighbours(axis):
    count = lax.axis_size(axis)
    up = [(i, i + 1) for i in range(count - 1)]
    return up, [(j, i) for i, j in up]


def shards(
    outline, centres, velocity, mass, response, pairs, pair_count, forcing, ocean_dest, ocean_floe
):
    rows_x, cols_y, span = outline.shape
    rows_dev, row_width = forcing.shape
    nx, ny = lax.axis_size("gx"), lax.axis_size("gy")
    devices = nx * ny
    floes = rows_x * cols_y
    cap = up_to(max(2, 5 * rows_dev // (2 * devices)), 16)
    params = pltpu.CompilerParams(vmem_limit_bytes=VMEM_BYTES)

    send = pl.pallas_call(
        functools.partial(pack_kernel, devices, cap, cols_y),
        out_shape=jax.ShapeDtypeStruct((devices, cap + 8, row_width), jnp.float32),
        in_specs=[in_vmem()] * 3,
        out_specs=in_vmem(),
        scratch_shapes=[
            pltpu.VMEM((1, rows_dev), jnp.int32),
            pltpu.VMEM((rows_dev, 2 * row_width), jnp.bfloat16),
            pltpu.VMEM((16, rows_dev), jnp.bfloat16),
        ],
        compiler_params=params,
        name="ocean_pack",
    )(ocean_dest.reshape(1, rows_dev), ocean_floe.reshape(1, rows_dev), forcing)
    got = lax.all_to_all(send, ("gx", "gy"), split_axis=0, concat_axis=0, tiled=True)

    up, down = neighbours("gx")
    north = lax.ppermute(outline[rows_x - 1], "gx", up)
    south = lax.ppermute(outline[0], "gx", down)
    up, down = neighbours("gy")
    left = jnp.concatenate([north[None, 0], outline[:, 0], south[None, 0]], axis=0)
    right = jnp.concatenate([north[None, -1], outline[:, -1], south[None, -1]], axis=0)
    west = lax.ppermute(right, "gy", up)
    east = lax.ppermute(left, "gy", down)
    side = up_to(rows_x + 2, 8)
    fill = jnp.zeros((side - rows_x - 2, span), jnp.float32)
    rim = jnp.concatenate([north, south, west, fill, east, fill], axis=0)

    lists = pairs[0, 0]
    slots = lists.shape[0]
    local = jnp.clip(lists[:, 0], 0, floes - 1)
    code = lists[:, 1]
    step_x = table_pick(code, DIRX)
    step_y = table_pick(code, DIRY)
    row = local // cols_y
    col = local % cols_y
    prow = row + step_x
    pcol = col + step_y
    glob_row = lax.axis_index("gx") * rows_x + prow
    glob_col = lax.axis_index("gy") * cols_y + pcol
    inside = (
        (glob_row >= 0) & (glob_row < rows_x * nx) & (glob_col >= 0) & (glob_col < cols_y * ny)
    )
    valid = (jnp.arange(slots, dtype=jnp.int32) < pair_count[0, 0]) & inside
    lines = floes + 2 * cols_y
    other = jnp.where(
        pcol < 0,
        lines + prow + 1,
        jnp.where(
            pcol >= cols_y,
            lines + side + prow + 1,
            jnp.where(
                prow < 0,
                floes + pcol,
                jnp.where(prow >= rows_x, floes + cols_y + pcol, prow * cols_y + pcol),
            ),
        ),
    )
    tiles = jnp.clip(lists[:, 2:], 0, 1)
    index = jnp.stack([local, tiles[:, 0], other, tiles[:, 1]], axis=0)
    nil = jnp.zeros_like(row)
    meta = jnp.stack(
        [row + 1, col + 1, prow + 1, pcol + 1, valid.astype(jnp.int32), step_x, step_y, nil], axis=0
    )
    tile_shape = jax.ShapeDtypeStruct((TILE, slots), jnp.float32)
    tile_sets = pl.pallas_call(
        gather_kernel,
        out_shape=[tile_shape] * 4,
        in_specs=[
            pl.BlockSpec(memory_space=pltpu.SMEM),
            pl.BlockSpec(memory_space=pl.ANY),
            pl.BlockSpec(memory_space=pl.ANY),
        ],
        out_specs=[in_vmem()] * 4,
        scratch_shapes=[pltpu.VMEM((floes + rim.shape[0], span), jnp.float32)]
        + [pltpu.VMEM((slots, TILE), jnp.float32)] * 4
        + [pltpu.SemaphoreType.DMA((2,))],
        compiler_params=params,
        name="gather_tiles",
    )(index, outline.reshape(floes, span), rim)

    names = got[:, cap:, :].reshape(devices, -1)[:, :cap].reshape(1, -1).astype(jnp.int32)
    ocean = pl.pallas_call(
        functools.partial(ocean_kernel, devices, cap),
        out_shape=jax.ShapeDtypeStruct((8, floes), jnp.float32),
        in_specs=[in_vmem()] * 3,
        out_specs=in_vmem(),
        scratch_shapes=[pltpu.VMEM((devices * cap, 2 * row_width), jnp.bfloat16)],
        compiler_params=params,
        name="ocean_force",
    )(names, got, response.reshape(floes, -1))
    ocean = ocean[:2].reshape(2, rows_x, cols_y)

    high = up_to(rows_x + 2, 8)
    state = jnp.concatenate(
        [
            jnp.moveaxis(centres, 2, 0),
            jnp.moveaxis(velocity, 2, 0),
            mass[None],
            ocean,
            jnp.zeros((1, rows_x, cols_y), jnp.float32),
        ],
        axis=0,
    )
    state = jnp.pad(state, ((0, 0), (1, high - rows_x - 1), (1, 128 - cols_y - 1)))
    grid = (high, 128)
    out = pl.pallas_call(
        functools.partial(steps_kernel, nx, ny, rows_x, cols_y),
        out_shape=jax.ShapeDtypeStruct((4,) + grid, jnp.float32),
        in_specs=[in_vmem()] * 6,
        out_specs=in_vmem(),
        scratch_shapes=[pltpu.VMEM((TILE, slots), jnp.float32)] * 5
        + [
            pltpu.VMEM((high, 2 * slots), jnp.float32),
            pltpu.VMEM((128, 2 * slots), jnp.float32),
            pltpu.VMEM((8, slots), jnp.float32),
            pltpu.VMEM((8,) + grid, jnp.float32),
            pltpu.VMEM((2,) + grid, jnp.float32),
            pltpu.VMEM((STEPS, 2) + grid, jnp.float32),
            pltpu.VMEM((6, 8, 8, 128), jnp.float32),
            pltpu.VMEM((2, 8) + grid, jnp.float32),
            pltpu.VMEM((STEPS, 6, 2, 8, 128), jnp.float32),
            pltpu.VMEM((STEPS, 2, 2) + grid, jnp.float32),
            pltpu.SemaphoreType.DMA((STEPS + 1, 8)),
            pltpu.SemaphoreType.DMA((STEPS + 1, 8)),
        ],
        compiler_params=pltpu.CompilerParams(
            vmem_limit_bytes=VMEM_BYTES, collective_id=0, has_side_effects=True
        ),
        name="contact_steps",
    )(*tile_sets, meta, state)
    out = out[:, 1 : rows_x + 1, 1 : cols_y + 1]
    return jnp.moveaxis(out[2:4], 0, 2), jnp.moveaxis(out[0:2], 0, 2)


def solution(mesh):
    return jax.shard_map(
        shards,
        mesh=mesh,
        in_specs=(
            P("gx", "gy", None),
            P("gx", "gy", None),
            P("gx", "gy", None),
            P("gx", "gy"),
            P("gx", "gy", None),
            P("gx", "gy", None, None),
            P("gx", "gy"),
            P(("gx", "gy"), None),
            P(("gx", "gy"), None),
            P(("gx", "gy")),
        ),
        out_specs=(P("gx", "gy", None), P("gx", "gy", None)),
        check_vma=False,
    )
```

time: 515 us -> 185 us (0.36); the launches traced: 507 us -> 184 us
  other arithmetic: 193 us -> 0.21 us
  local copies, waits for them, and re-layouts: 186 us -> 19.4 us
  Pallas kernels: 0 us -> 108 us
  starting transfers between devices: 76.3 us -> 17.9 us
  matrix products: 15.3 us -> 0 us
    pallas_call x0 -> x4, Pallas kernels: none -> 108 us  [the longest x1 75.4 us: shards(): pl.pallas_call(functools.partial(steps_kernel, nx, ny, rows_x, cols_y), o...]
    reduce_sum x7 -> x0, other arithmetic: 89.9 us -> none  [the longest x6 89.8 us: tile_force(): jnp.sum(weight * diff_x, axis=(1, 2))]
    scatter-add x7 -> x0, other arithmetic: 53.2 us -> none  [the longest x1 34.4 us: shards(): ocean_sum = jnp.zeros((rows_x * cols_y, row_width), jnp.float32).at[floe_...]
    ppermute x24 -> x4, starting transfers between devices: 63.1 us -> 11.4 us  [the longest x1 3.6 us: shards(): west = lax.ppermute(right, 'gy', up)]
    while x3 -> x0, local copies, waits for them, and re-layouts: 45.6 us -> none  [tile_terms(): lax.map(block, (shaped(own_key), shaped(other_key), shaped(step_x), shape...]
    reshape x13 -> x1, local copies, waits for them, and re-layouts: 42.1 us -> 0.12 us  [shards(): ocean = ocean[:2].reshape(2, rows_x, cols_y)]
    gather x12 -> x0, local copies, waits for them, and re-layouts: 39.5 us -> none  [the longest x6 19.8 us: block(): own = jnp.take(rows_table, ok_own, axis=0)]
    another operation x7 -> x2, other arithmetic: 16.1 us -> 0.03 us  [shards(): index = jnp.stack([local, tiles[:, 0], other, tiles[:, 1]], axis=0)]
  transfers between devices with their start and end apart: 26 -> 5, of which waited for: 11 -> 5; matrix products, arithmetic and copies ran while one was open for 23% -> 2% of each run, Pallas kernels for 0% -> 3%
where the time goes in v1:
time: 185 us; the launch traced here: 184 us
  Pallas kernels  108 us (58%)
  waiting for transfers between devices  36.7 us (20%)
  local copies, waits for them, and re-layouts  19.4 us (10%)
  starting transfers between devices  17.9 us (10%)
    pallas_call x1, Pallas kernels, shards(): pl.pallas_call(functools.partial(steps_kernel, nx, ny, rows_x, cols_y), o...  75.4 us
    pallas_call x1, Pallas kernels, shards(): pl.pallas_call(functools.partial(pack_kernel, devices, cap, cols_y), out_...  16.3 us
    ppermute x1, waiting for transfers between devices, shards(): west = lax.ppermute(right, 'gy', up)  16 us
    unnamed x49, local copies, waits for them, and re-layouts  13.5 us
    pallas_call x1, Pallas kernels, shards(): pl.pallas_call(functools.partial(ocean_kernel, devices, cap), out_shape=j...  10.4 us
    ppermute x1, waiting for transfers between devices, shards(): east = lax.ppermute(left, 'gy', down)  6.86 us
    ppermute x1, waiting for transfers between devices, shards(): north = lax.ppermute(outline[rows_x - 1], 'gx', up)  6.56 us
    all_to_all x1, starting transfers between devices, shards(): lax.all_to_all(send, ('gx', 'gy'), split_axis=0, concat_axis=0, tiled=True)  6.45 us
  transfers between devices with their start and end apart: 5, of which 5 were waited for; matrix products, arithmetic and copies ran while one was open for 2% of the time, Pallas kernels for 3%

profile of v1, /device:TPU:3, one launch (start us, length us, event | category | flops | bytes accessed | tf_op | source)
XLA Modules:
  0.0 184.2 jit_solution(13038631971371309796)
XLA Ops:
  0.6 1.2 copy-done.3
  3.3 16.3 %ocean_pack.1 = f32[32,168,128]{2,1,0:T(8,128)S(1)} custom-call(s32[1,2048]{1,0:T(1,128)S(1)} %bitcast.48, s32[1,2048]{1,0:T(1,128)S(1)} %bitcast.49, f32[2048,128]{1,0:T(8,128)S(1)} %copy-done.3), custom_call_target="tpu_custom_call" | custom-call | tf_op jit(solution)/shard_map/ocean_pack/pallas_call | solution.py:347
  19.5 1.5 copy-done
  21.1 6.4 %all-to-all-start = ((f32[32,168,128]{2,1,0:T(8,128)}), f32[32,168,128]{2,1,0:T(8,128)S(1)}, u32[]{:S(2)}, u32[]{:S(2)}) async-start(f32[32,168,128]{2,1,0:T(8,128)} %copy-done), calls=%async_computation | async-start | bytes 5505024 | tf_op jit(solution)/shard_map/all_to_all | solution.py:360
  27.6 1.7 slice_bitcast_fusion
  29.2 3.3 %collective-permute-start = (f32[64,512]{1,0:T(8,128)}, f32[64,512]{1,0:T(8,128)S(1)}, u32[]{:S(2)}, u32[]{:S(2)}) collective-permute-start(f32[64,512]{1,0:T(8,128)} %get-tuple-element.22), channel_id=1, source_target_pairs={{0,8},{8,16},{16,24},{1,9},{9,17},{17,25},{2,10},{10,18},{18,26},{... | collective-permute-start | bytes 393224 | tf_op jit(solution)/shard_map/ppermute | solution.py:363
  32.6 1.9 %collective-permute-start.1 = (f32[64,512]{1,0:T(8,128)}, f32[64,512]{1,0:T(8,128)S(1)}, u32[]{:S(2)}, u32[]{:S(2)}) collective-permute-start(f32[64,512]{1,0:T(8,128)} %get-tuple-element.21), channel_id=1, source_target_pairs={{8,0},{16,8},{24,16},{9,1},{17,9},{25,17},{10,2},{18,10},{26,18},{... | collective-permute-start | bytes 393224 | tf_op jit(solution)/shard_map/ppermute | solution.py:364
  35.2 1.3 fusion.1
  36.9 6.6 %collective-permute-done = f32[64,512]{1,0:T(8,128)S(1)} collective-permute-done((f32[64,512]{1,0:T(8,128)}, f32[64,512]{1,0:T(8,128)S(1)}, u32[]{:S(2)}, u32[]{:S(2)}) %collective-permute-start) | collective-permute-done | bytes 131104 | tf_op jit(solution)/shard_map/ppermute | solution.py:363
  43.4 2.0 %collective-permute-done.1 = f32[64,512]{1,0:T(8,128)S(1)} collective-permute-done((f32[64,512]{1,0:T(8,128)}, f32[64,512]{1,0:T(8,128)S(1)}, u32[]{:S(2)}, u32[]{:S(2)}) %collective-permute-start.1) | collective-permute-done | bytes 131104 | tf_op jit(solution)/shard_map/ppermute | solution.py:364
  45.5 2.6 %collective-permute-start.3 = (f32[34,512]{1,0:T(8,128)S(1)}, f32[34,512]{1,0:T(8,128)S(1)}, u32[]{:S(2)}, u32[]{:S(2)}) collective-permute-start(f32[34,512]{1,0:T(8,128)S(1)} %pad_maximum_fusion.1), channel_id=1, source_target_pairs={{1,0},{2,1},{3,2},{4,3},{5,4},{6,5},{7,6},{9,8},{10,9},{11,10},{12... | collective-permute-start | bytes 208904 | tf_op jit(solution)/shard_map/ppermute | solution.py:369
  48.1 3.6 %collective-permute-start.2 = (f32[34,512]{1,0:T(8,128)S(1)}, f32[34,512]{1,0:T(8,128)S(1)}, u32[]{:S(2)}, u32[]{:S(2)}) collective-permute-start(f32[34,512]{1,0:T(8,128)S(1)} %pad_maximum_fusion), channel_id=1, source_target_pairs={{0,1},{1,2},{2,3},{3,4},{4,5},{5,6},{6,7},{8,9},{9,10},{10,11},{11... | collective-permute-start | bytes 208904 | tf_op jit(solution)/shard_map/ppermute | solution.py:368
  51.7 6.9 %collective-permute-done.3 = f32[34,512]{1,0:T(8,128)S(1)} collective-permute-done((f32[34,512]{1,0:T(8,128)S(1)}, f32[34,512]{1,0:T(8,128)S(1)}, u32[]{:S(2)}, u32[]{:S(2)}) %collective-permute-start.3) | collective-permute-done | bytes 69664 | tf_op jit(solution)/shard_map/ppermute | solution.py:369
  58.6 16.0 %collective-permute-done.2 = f32[34,512]{1,0:T(8,128)S(1)} collective-permute-done((f32[34,512]{1,0:T(8,128)S(1)}, f32[34,512]{1,0:T(8,128)S(1)}, u32[]{:S(2)}, u32[]{:S(2)}) %collective-permute-start.2) | collective-permute-done | bytes 69664 | tf_op jit(solution)/shard_map/ppermute | solution.py:368
  74.6 1.0 concatenate.14.rim_ref
  75.6 2.2 %copy-done.1 = f32[32,64,512]{2,1,0:T(8,128)S(1)} copy-done((f32[32,64,512]{2,1,0:T(8,128)S(1)}, f32[32,64,512]{2,1,0:T(8,128)}, u32[]{:S(2)}) %copy-start.1) | copy-done | bytes 4194328
  77.8 6.2 %gather_tiles.1 = (f32[128,512]{1,0:T(8,128)S(1)}, f32[128,512]{1,0:T(8,128)S(1)}, f32[128,512]{1,0:T(8,128)S(1)}, f32[128,512]{1,0:T(8,128)S(1)}) custom-call(s32[4,512]{1,0:T(4,128)S(1)} %pad_add_fusion.index_ref, f32[2048,512]{1,0:T(8,128)S(1)} %bitcast.46, f32[208,512]{1,0:T(8,128)S(1)} %concatenate.14.rim_ref), custom_call_target="tpu_custom_call" | custom-call | tf_op jit(solution)/shard_map/gather_tiles/pallas_call | solution.py:411
  86.1 5.2 %all-to-all-done.rows_ref = f32[32,168,128]{2,1,0:T(8,128)S(1)} async-done(((f32[32,168,128]{2,1,0:T(8,128)}), f32[32,168,128]{2,1,0:T(8,128)S(1)}, u32[]{:S(2)}, u32[]{:S(2)}) %all-to-all-start) | async-done | bytes 2752544 | tf_op jit(solution)/shard_map/all_to_all | solution.py:360
  91.5 1.2 copy-done.2
  92.7 10.4 %ocean_force.1 = f32[8,2048]{1,0:T(8,128)S(1)} custom-call(s32[1,5120]{1,0:T(1,128)S(1)} %convert_element_type.19.index_ref, f32[32,168,128]{2,1,0:T(8,128)S(1)} %all-to-all-done.rows_ref, f32[2048,64]{1,0:T(8,128)S(1)} %bitcast.47), custom_call_target="tpu_custom_call" | custom-call | tf_op jit(solution)/shard_map/ocean_force/pallas_call | solution.py:428
  104.4 1.0 pad.4.state_ref
  105.5 0.9 copy-done.7
  106.4 0.9 copy-done.9
  107.3 75.4 %contact_steps.1 = f32[4,40,128]{2,1,0:T(8,128)S(1)} custom-call(f32[128,512]{1,0:T(8,128)S(1)} %get-tuple-element.6.ox_ref, f32[128,512]{1,0:T(8,128)S(1)} %copy-done.5, f32[128,512]{1,0:T(8,128)S(1)} %copy-done.7, f32[128,512]{1,0:T(8,128)S(1)} %copy-done.9, s32[8,512]{1,0:T(8,128)S(1)} %stack.5.meta_ref, f32[8,40,128]{2,1,0:T(8,128)S(1)} %pad.4.state_ref), custom_call_target="tpu_custom_call" | custom-call | tf_op jit(solution)/shard_map/contact_steps/pallas_call | solution.py:452
  (63 shorter events, 6.7 us)
Async XLA Ops:
  0.6 1.2 copy-start.3
  1.9 0.7 copy-start.10
  2.6 0.7 copy-start.11
  19.5 1.5 copy-start
  21.1 15.4 %copy-start.17 = (s32[1,1,512,4]{2,3,1,0:T(4,128)S(1)}, s32[1,1,512,4]{2,3,1,0:T(4,128)}, u32[]{:S(2)}) copy-start(s32[1,1,512,4]{2,3,1,0:T(4,128)} %param.17) | copy-start | bytes 24580
  21.1 15.5 %copy-start.18 = (s32[8]{0:T(128)S(1)}, s32[8]{0:T(128)}, u32[]{:S(2)}) copy-start(s32[8]{0:T(128)} %constant.69.clone) | copy-start | bytes 100
  21.1 15.5 %copy-start.19 = (s32[8]{0:T(128)S(1)}, s32[8]{0:T(128)}, u32[]{:S(2)}) copy-start(s32[8]{0:T(128)} %constant.70.clone) | copy-start | bytes 100
  21.1 15.7 %copy-start.14 = (f32[32,64,2]{1,2,0:T(2,128)S(1)}, f32[32,64,2]{1,2,0:T(2,128)}, u32[]{:S(2)}) copy-start(f32[32,64,2]{1,2,0:T(2,128)} %param.13) | copy-start | bytes 49156
  21.1 15.7 %copy-start.15 = (f32[32,64,2]{1,2,0:T(2,128)S(1)}, f32[32,64,2]{1,2,0:T(2,128)}, u32[]{:S(2)}) copy-start(f32[32,64,2]{1,2,0:T(2,128)} %param.14) | copy-start | bytes 49156
  21.1 15.7 %copy-start.16 = (f32[32,64]{1,0:T(8,128)S(1)}, f32[32,64]{1,0:T(8,128)}, u32[]{:S(2)}) copy-start(f32[32,64]{1,0:T(8,128)} %param.15) | copy-start | bytes 24580
  21.1 70.2 %all-to-all-start = ((f32[32,168,128]{2,1,0:T(8,128)}), f32[32,168,128]{2,1,0:T(8,128)S(1)}, u32[]{:S(2)}, u32[]{:S(2)}) async-start(f32[32,168,128]{2,1,0:T(8,128)} %copy-done), calls=%async_computation | async-start | bytes 5505024 | tf_op jit(solution)/shard_map/all_to_all | solution.py:360
  29.2 14.2 %collective-permute-start = (f32[64,512]{1,0:T(8,128)}, f32[64,512]{1,0:T(8,128)S(1)}, u32[]{:S(2)}, u32[]{:S(2)}) collective-permute-start(f32[64,512]{1,0:T(8,128)} %get-tuple-element.22), channel_id=1, source_target_pairs={{0,8},{8,16},{16,24},{1,9},{9,17},{17,25},{2,10},{10,18},{18,26},{... | collective-permute-start | bytes 393224 | tf_op jit(solution)/shard_map/ppermute | solution.py:363
  32.6 12.9 %collective-permute-start.1 = (f32[64,512]{1,0:T(8,128)}, f32[64,512]{1,0:T(8,128)S(1)}, u32[]{:S(2)}, u32[]{:S(2)}) collective-permute-start(f32[64,512]{1,0:T(8,128)} %get-tuple-element.21), channel_id=1, source_target_pairs={{8,0},{16,8},{24,16},{9,1},{17,9},{25,17},{10,2},{18,10},{26,18},{... | collective-permute-start | bytes 393224 | tf_op jit(solution)/shard_map/ppermute | solution.py:364
  36.9 37.8 %copy-start.12 = (f32[8,32,64]{2,1,0:T(8,128)}, f32[8,32,64]{2,1,0:T(8,128)S(1)}, u32[]{:S(2)}) copy-start(f32[8,32,64]{2,1,0:T(8,128)S(1)} %bitcast_dynamic-update-slice_fusion.2) | copy-start | bytes 196612
  45.5 29.2 %copy-start.13 = (f32[64,512]{1,0:T(8,128)}, f32[64,512]{1,0:T(8,128)S(1)}, u32[]{:S(2)}) copy-start(f32[64,512]{1,0:T(8,128)S(1)} %collective-permute-done.1) | copy-start | bytes 393220
  45.5 13.1 %collective-permute-start.3 = (f32[34,512]{1,0:T(8,128)S(1)}, f32[34,512]{1,0:T(8,128)S(1)}, u32[]{:S(2)}, u32[]{:S(2)}) collective-permute-start(f32[34,512]{1,0:T(8,128)S(1)} %pad_maximum_fusion.1), channel_id=1, source_target_pairs={{1,0},{2,1},{3,2},{4,3},{5,4},{6,5},{7,6},{9,8},{10,9},{11,10},{12... | collective-permute-start | bytes 208904 | tf_op jit(solution)/shard_map/ppermute | solution.py:369
  48.1 26.5 %collective-permute-start.2 = (f32[34,512]{1,0:T(8,128)S(1)}, f32[34,512]{1,0:T(8,128)S(1)}, u32[]{:S(2)}, u32[]{:S(2)}) collective-permute-start(f32[34,512]{1,0:T(8,128)S(1)} %pad_maximum_fusion), channel_id=1, source_target_pairs={{0,1},{1,2},{2,3},{3,4},{4,5},{5,6},{6,7},{8,9},{9,10},{10,11},{11... | collective-permute-start | bytes 208904 | tf_op jit(solution)/shard_map/ppermute | solution.py:368
  75.6 2.2 %copy-start.1 = (f32[32,64,512]{2,1,0:T(8,128)S(1)}, f32[32,64,512]{2,1,0:T(8,128)}, u32[]{:S(2)}) copy-start(f32[32,64,512]{2,1,0:T(8,128)} %param.12) | copy-start | bytes 12582916
  84.0 0.7 copy-start.4
  85.4 0.7 copy-start.8
  91.3 14.1 %copy-start.5 = (f32[128,512]{1,0:T(8,128)S(1)}, f32[128,512]{1,0:T(8,128)}, u32[]{:S(2)}) copy-start(f32[128,512]{1,0:T(8,128)} %copy-done.4) | copy-start | bytes 786436
  91.5 1.2 copy-start.2
  105.4 1.0 copy-start.7
  106.4 0.9 copy-start.9
  (1 other events, 0.7 us)

commit v2 on v1

--- a/solution.py
+++ b/solution.py
@@ -41,7 +41,7 @@
     return pl.BlockSpec(memory_space=pltpu.VMEM)
 
 
-def pack_kernel(devices, cap, cols, dest_ref, floe_ref, rows_ref, out_ref, place, halves, names):
+def pack_kernel(devices, cap, cols, dest_ref, floe_ref, rows_ref, out_ref, place, rank, halves, local):
     count = dest_ref.shape[1]
     width = 256
     before = hot(
@@ -55,31 +55,42 @@
         match = owner == dest
         earlier = jnp.dot(hot(match), before, preferred_element_type=jnp.float32) + offset
         slot = jnp.sum(jnp.where(match, earlier, 0.0), axis=0, keepdims=True)
+        rank[:, start : start + width] = slot.astype(jnp.int32)
         place[:, start : start + width] = dest * cap + slot.astype(jnp.int32)
         offset = offset + jnp.sum(jnp.where(match, 1.0, 0.0), axis=1, keepdims=True)
     halves[...] = split_two(rows_ref[...])
     floe = floe_ref[...]
-    names[...] = jnp.concatenate(
-        [(floe // cols).astype(jnp.float32), (floe % cols).astype(jnp.float32)]
-        + [jnp.zeros((1, count), jnp.float32)] * 14,
+    match = lax.broadcasted_iota(jnp.int32, (devices, count), 0) == dest_ref[...]
+    named = jnp.concatenate(
+        [
+            jnp.where(match, (floe // cols).astype(jnp.float32), 0.0),
+            jnp.where(match, (floe % cols).astype(jnp.float32), 0.0),
+        ],
         axis=0,
     ).astype(jnp.bfloat16)
-
-    def one(device, carry):
-        slots = lax.broadcasted_iota(jnp.int32, (cap, count), 0) + device * cap
+    ranked = hot(lax.broadcasted_iota(jnp.int32, (cap, count), 0) == rank[...])
+    name = lax.dot_general(named, ranked, NT, preferred_element_type=jnp.float32)
+    local[...] = name[:devices] * float(cols) + name[devices:]
+    group = math.gcd(devices, 4)
+
+    def one(turn, carry):
+        first = turn * group
+        slots = lax.broadcasted_iota(jnp.int32, (group * cap, count), 0) + first * cap
         chosen = hot(slots == place[...])
         both = jnp.dot(chosen, halves[...], preferred_element_type=jnp.float32)
-        out_ref[device, 0:cap, :] = both[:, :128] + both[:, 128:]
-        name = lax.dot_general(names[...], chosen, NT, preferred_element_type=jnp.float32)
-        local = name[0:1] * float(cols) + name[1:2]
-        out_ref[device, cap : cap + 8, :] = jnp.zeros((8, 128), jnp.float32)
-        for start in range(0, cap, 128):
-            size = min(128, cap - start)
-            line = cap + start // 128
-            out_ref[device, line : line + 1, 0:size] = local[:, start : start + size]
+        both = both[:, :128] + both[:, 128:]
+        for part in range(group):
+            device = first + part
+            out_ref[device, 0:cap, :] = both[part * cap : (part + 1) * cap]
+            out_ref[device, cap : cap + 8, :] = jnp.zeros((8, 128), jnp.float32)
+            mine = local[pl.ds(device, 1), :]
+            for start in range(0, cap, 128):
+                size = min(128, cap - start)
+                line = cap + start // 128
+                out_ref[device, line : line + 1, 0:size] = mine[:, start : start + size]
         return carry
 
-    lax.fori_loop(0, devices, one, 0)
+    lax.fori_loop(0, devices // group, one, 0)
 
 
 def ocean_kernel(devices, cap, index_ref, rows_ref, response_ref, out_ref, halves):
@@ -142,11 +153,20 @@
             out[:, start : start + 128] = source[start : start + 128, :].T
 
 
-def steps_kernel(
-    nx, ny, rows, cols, ox_ref, oy_ref, px_ref, py_ref, meta_ref, state_ref, out_ref,
-    px2, py2, pq, ax_ref, ay_ref, own_row, own_col, force, state, total, sums,
-    first_line, first_side, later_line, later_side, send_sem, recv_sem,
-):
+def steps_kernel(nx, ny, rows, cols, opening, ox_ref, oy_ref, px_ref, py_ref, meta_ref, state_ref, *refs):
+    if opening:
+        state_out, total_out = refs[:2]
+        refs = refs[2:]
+        first_sent = state_ref
+    else:
+        wave_ref, contact_ref, out_ref = refs[:3]
+        refs = refs[3:]
+        first_sent = wave_ref
+    (
+        px2, py2, pq, ax_ref, ay_ref, own_row, own_col, force, state, wave, total, sums,
+        first_line, first_side, later_line, later_side, send_sem, recv_sem,
+    ) = refs
+    steps = 1 if opening else STEPS - 1
     my_x = lax.axis_index("gx")
     my_y = lax.axis_index("gy")
     slots = ox_ref.shape[1]
@@ -222,8 +242,10 @@
                         piece = pltpu.roll(piece, (cols if dy < 0 else 128 - cols), 1)
                     into[part, top : top + size, :] += jnp.where(keep, piece, 0.0)
 
-    send(0, state_ref)
+    send(0, first_sent)
     state[...] = state_ref[...]
+    if not opening:
+        wave[...] = wave_ref[...]
 
     px = px_ref[...] * SCALE
     py = py_ref[...] * SCALE
@@ -242,12 +264,25 @@
     valid = meta[4:5] > 0
     step_x = meta[5:6].astype(jnp.float32)
     step_y = meta[6:7].astype(jnp.float32)
-    collect(0, state_ref, state)
-    mass = jnp.where(state[4] == 0.0, 1.0, state[4])
+
+    def advance(contact):
+        mass = jnp.where(state[4] == 0.0, 1.0, state[4])
+        for axis in range(2):
+            vel = state[2 + axis]
+            vel = vel + DT * ((contact[axis] + wave[axis]) - DRAG * vel) / mass
+            state[2 + axis] = vel
+            state[axis] = state[axis] + DT * vel
+
+    if opening:
+        collect(0, state_ref, state)
+        state_out[...] = state[...]
+    else:
+        collect(0, wave_ref, wave)
+        advance(contact_ref)
 
     tall = 64
 
-    for step in range(STEPS):
+    for step in range(steps):
         shift = jnp.concatenate([state[0], state[1]], axis=0)
         picked = jnp.dot(shift, own_col[...], precision=EXACT, preferred_element_type=jnp.float32)
         at_x = jnp.sum(picked[:high] * own_row[...], axis=0, keepdims=True)
@@ -307,18 +342,18 @@
         total[0] = placed[:high]
         total[1] = placed[high:]
         collect(step + 1, mine, total)
-        for axis in range(2):
-            vel = state[2 + axis]
-            vel = vel + DT * ((total[axis] + state[5 + axis]) - DRAG * vel) / mass
-            state[2 + axis] = vel
-            state[axis] = state[axis] + DT * vel
-
-    out_ref[...] = state[0:4]
-    for turn in range(STEPS + 1):
+        if not opening:
+            advance(total)
+
+    if opening:
+        total_out[...] = total[...]
+    else:
+        out_ref[...] = state[0:4]
+    for turn in range(steps + 1):
         for way in range(8):
             @pl.when(present(DIRX[way], DIRY[way]))
             def _():
-                source = state_ref if turn == 0 else sums.at[turn - 1]
+                source = first_sent if turn == 0 else sums.at[turn - 1]
                 descriptor(turn, way, source, 1).wait_send()
 
 
@@ -351,14 +386,16 @@
         out_specs=in_vmem(),
         scratch_shapes=[
             pltpu.VMEM((1, rows_dev), jnp.int32),
+            pltpu.VMEM((1, rows_dev), jnp.int32),
             pltpu.VMEM((rows_dev, 2 * row_width), jnp.bfloat16),
-            pltpu.VMEM((16, rows_dev), jnp.bfloat16),
+            pltpu.VMEM((devices, cap), jnp.float32),
         ],
+        cost_estimate=pl.CostEstimate(
+            flops=4 * devices * cap * rows_dev * row_width, bytes_accessed=10**7, transcendentals=0
+        ),
         compiler_params=params,
         name="ocean_pack",
     )(ocean_dest.reshape(1, rows_dev), ocean_floe.reshape(1, rows_dev), forcing)
-    got = lax.all_to_all(send, ("gx", "gy"), split_axis=0, concat_axis=0, tiled=True)
-
     up, down = neighbours("gx")
     north = lax.ppermute(outline[rows_x - 1], "gx", up)
     south = lax.ppermute(outline[0], "gx", down)
@@ -370,6 +407,8 @@
     side = up_to(rows_x + 2, 8)
     fill = jnp.zeros((side - rows_x - 2, span), jnp.float32)
     rim = jnp.concatenate([north, south, west, fill, east, fill], axis=0)
+    rim, send = lax.optimization_barrier((rim, send))
+    got = lax.all_to_all(send, ("gx", "gy"), split_axis=0, concat_axis=0, tiled=True)
 
     lists = pairs[0, 0]
     slots = lists.shape[0]
@@ -424,6 +463,67 @@
         name="gather_tiles",
     )(index, outline.reshape(floes, span), rim)
 
+    high = up_to(rows_x + 2, 8)
+    grid = (high, 128)
+
+    def rimmed(parts):
+        return jnp.pad(parts, ((0, 0), (1, high - rows_x - 1), (1, 128 - cols_y - 1)))
+
+    def contact_call(opening, out_shape, *operands):
+        steps = 1 if opening else STEPS - 1
+        sent = 8 if opening else 2
+        return pl.pallas_call(
+            functools.partial(steps_kernel, nx, ny, rows_x, cols_y, opening),
+            out_shape=out_shape,
+            in_specs=[in_vmem()] * len(operands),
+            out_specs=jax.tree.map(lambda _: in_vmem(), out_shape),
+            scratch_shapes=[pltpu.VMEM((TILE, slots), jnp.float32)] * 5
+            + [
+                pltpu.VMEM((high, 2 * slots), jnp.float32),
+                pltpu.VMEM((128, 2 * slots), jnp.float32),
+                pltpu.VMEM((8, slots), jnp.float32),
+                pltpu.VMEM((8,) + grid, jnp.float32),
+                pltpu.VMEM((2,) + grid, jnp.float32),
+                pltpu.VMEM((2,) + grid, jnp.float32),
+                pltpu.VMEM((steps, 2) + grid, jnp.float32),
+                pltpu.VMEM((6, sent, 8, 128), jnp.float32),
+                pltpu.VMEM((2, sent) + grid, jnp.float32),
+                pltpu.VMEM((steps, 6, 2, 8, 128), jnp.float32),
+                pltpu.VMEM((steps, 2, 2) + grid, jnp.float32),
+                pltpu.SemaphoreType.DMA((steps + 1, 8)),
+                pltpu.SemaphoreType.DMA((steps + 1, 8)),
+            ],
+            cost_estimate=pl.CostEstimate(
+                flops=steps * 10 * slots * TILE * TILE,
+                bytes_accessed=10**8,
+                transcendentals=steps * slots * TILE * TILE,
+            ),
+            compiler_params=pltpu.CompilerParams(
+                vmem_limit_bytes=VMEM_BYTES,
+                collective_id=0 if opening else 1,
+                has_side_effects=True,
+            ),
+            name="contact_opening" if opening else "contact_steps",
+        )(*operands)
+
+    state = rimmed(
+        jnp.concatenate(
+            [
+                jnp.moveaxis(centres, 2, 0),
+                jnp.moveaxis(velocity, 2, 0),
+                mass[None],
+                jnp.zeros((3, rows_x, cols_y), jnp.float32),
+            ],
+            axis=0,
+        )
+    )
+    state, contact = contact_call(
+        True,
+        [jax.ShapeDtypeStruct((n,) + grid, jnp.float32) for n in (8, 2)],
+        *tile_sets, meta, state,
+    )
+
+    response, contact = lax.optimization_barrier((response, contact))
     names = got[:, cap:, :].reshape(devices, -1)[:, :cap].reshape(1, -1).astype(jnp.int32)
     ocean = pl.pallas_call(
         functools.partial(ocean_kernel, devices, cap),
@@ -436,44 +536,11 @@
     )(names, got, response.reshape(floes, -1))
     ocean = ocean[:2].reshape(2, rows_x, cols_y)
 
-    high = up_to(rows_x + 2, 8)
-    state = jnp.concatenate(
-        [
-            jnp.moveaxis(centres, 2, 0),
-            jnp.moveaxis(velocity, 2, 0),
-            mass[None],
-            ocean,
-            jnp.zeros((1, rows_x, cols_y), jnp.float32),
-        ],
-        axis=0,
-    )
-    state = jnp.pad(state, ((0, 0), (1, high - rows_x - 1), (1, 128 - cols_y - 1)))
-    grid = (high, 128)
-    out = pl.pallas_call(
-        functools.partial(steps_kernel, nx, ny, rows_x, cols_y),
-        out_shape=jax.ShapeDtypeStruct((4,) + grid, jnp.float32),
-        in_specs=[in_vmem()] * 6,
-        out_specs=in_vmem(),
-        scratch_shapes=[pltpu.VMEM((TILE, slots), jnp.float32)] * 5
-        + [
-            pltpu.VMEM((high, 2 * slots), jnp.float32),
-            pltpu.VMEM((128, 2 * slots), jnp.float32),
-            pltpu.VMEM((8, slots), jnp.float32),
-            pltpu.VMEM((8,) + grid, jnp.float32),
-            pltpu.VMEM((2,) + grid, jnp.float32),
-            pltpu.VMEM((STEPS, 2) + grid, jnp.float32),
-            pltpu.VMEM((6, 8, 8, 128), jnp.float32),
-            pltpu.VMEM((2, 8) + grid, jnp.float32),
-            pltpu.VMEM((STEPS, 6, 2, 8, 128), jnp.float32),
-            pltpu.VMEM((STEPS, 2, 2) + grid, jnp.float32),
-            pltpu.SemaphoreType.DMA((STEPS + 1, 8)),
-            pltpu.SemaphoreType.DMA((STEPS + 1, 8)),
-        ],
-        compiler_params=pltpu.CompilerParams(
-            vmem_limit_bytes=VMEM_BYTES, collective_id=0, has_side_effects=True
-        ),
-        name="contact_steps",
-    )(*tile_sets, meta, state)
+    out = contact_call(
+        False,
+        jax.ShapeDtypeStruct((4,) + grid, jnp.float32),
+        *tile_sets, meta, state, rimmed(ocean), contact,
+    )
     out = out[:, 1 : rows_x + 1, 1 : cols_y + 1]
     return jnp.moveaxis(out[2:4], 0, 2), jnp.moveaxis(out[0:2], 0, 2)
 

time: 185 us -> 175 us (0.946)
  waiting for transfers between devices: 36.7 us -> 0.56 us
  Pallas kernels: 108 us -> 139 us
  local copies, waits for them, and re-layouts: 19.4 us -> 14.4 us
    pallas_call x1 -> x2, Pallas kernels: 75.4 us -> 115 us  [contact_call(): pl.pallas_call(functools.partial(steps_kernel, nx, ny, rows_x, cols_y, op...]
    ppermute x1, waiting for transfers between devices: 16 us -> 0.01 us  [shards(): west = lax.ppermute(right, 'gy', up)]
    pallas_call x1, Pallas kernels: 16.3 us -> 7.61 us  [shards(): pl.pallas_call(functools.partial(pack_kernel, devices, cap, cols_y), out_...]
    ppermute x1, waiting for transfers between devices: 6.86 us -> 0.01 us  [shards(): east = lax.ppermute(left, 'gy', down)]
    ppermute x1, waiting for transfers between devices: 6.56 us -> 0.55 us  [shards(): north = lax.ppermute(outline[rows_x - 1], 'gx', up)]
    all_to_all x1, waiting for transfers between devices: 5.22 us -> 0.01 us  [shards(): lax.all_to_all(send, ('gx', 'gy'), split_axis=0, concat_axis=0, tiled=True)]
    unnamed x49, local copies, waits for them, and re-layouts: 13.5 us -> 11.4 us
    ppermute x1, waiting for transfers between devices: 2.03 us -> 0.01 us  [shards(): south = lax.ppermute(outline[0], 'gx', down)]
  transfers between devices with their start and end apart: 5 -> 5, of which waited for: 5 -> 1; matrix products, arithmetic and copies ran while one was open for 2% -> 1% of each run, Pallas kernels for 3% -> 43%
where the time goes in v2:
time: 175 us; the launch traced here: 174 us
  Pallas kernels  139 us (79%)
  starting transfers between devices  18.6 us (11%)
  local copies, waits for them, and re-layouts  14.4 us (8%)
    pallas_call x2, Pallas kernels, contact_call(): pl.pallas_call(functools.partial(steps_kernel, nx, ny, rows_x, cols_y, op...  115 us
    unnamed x49, local copies, waits for them, and re-layouts  11.4 us
    pallas_call x1, Pallas kernels, shards(): pl.pallas_call(functools.partial(ocean_kernel, devices, cap), out_shape=j...  10.4 us
    all_to_all x1, starting transfers between devices, shards(): lax.all_to_all(send, ('gx', 'gy'), split_axis=0, concat_axis=0, tiled=True)  7.65 us
    pallas_call x1, Pallas kernels, shards(): pl.pallas_call(functools.partial(pack_kernel, devices, cap, cols_y), out_...  7.61 us
    pallas_call x1, Pallas kernels, shards(): pl.pallas_call(gather_kernel, out_shape=[tile_shape] * 4, in_specs=[pl.Bl...  6.21 us
  transfers between devices with their start and end apart: 5, of which 1 were waited for; matrix products, arithmetic and copies ran while one was open for 1% of the time, Pallas kernels for 43%

profile of v2, /device:TPU:3, one launch (start us, length us, event | category | flops | bytes accessed | tf_op | source)
XLA Modules:
  0.0 174.3 jit_solution(17833663435821993696)
XLA Ops:
  0.6 1.0 slice_bitcast_fusion
  1.6 2.6 %collective-permute-start.1 = (f32[64,512]{1,0:T(8,128)S(1)}, f32[64,512]{1,0:T(8,128)S(1)}, u32[]{:S(2)}, u32[]{:S(2)}) collective-permute-start(f32[64,512]{1,0:T(8,128)S(1)} %get-tuple-element.33), channel_id=1, source_target_pairs={{8,0},{16,8},{24,16},{9,1},{17,9},{25,17},{10,2},{18,10},{26,18},{... | collective-permute-start | bytes 393224 | tf_op jit(solution)/shard_map/ppermute | solution.py:401
  4.2 3.0 %collective-permute-start = (f32[64,512]{1,0:T(8,128)S(1)}, f32[64,512]{1,0:T(8,128)S(1)}, u32[]{:S(2)}, u32[]{:S(2)}) collective-permute-start(f32[64,512]{1,0:T(8,128)S(1)} %get-tuple-element.34), channel_id=1, source_target_pairs={{0,8},{8,16},{16,24},{1,9},{9,17},{17,25},{2,10},{10,18},{18,26},{... | collective-permute-start | bytes 393224 | tf_op jit(solution)/shard_map/ppermute | solution.py:400
  7.3 1.3 fusion.1
  8.6 0.6 collective-permute-done
  9.2 3.2 %collective-permute-start.2 = (f32[34,512]{1,0:T(8,128)S(1)}, f32[34,512]{1,0:T(8,128)S(1)}, u32[]{:S(2)}, u32[]{:S(2)}) collective-permute-start(f32[34,512]{1,0:T(8,128)S(1)} %pad_maximum_fusion), channel_id=1, source_target_pairs={{0,1},{1,2},{2,3},{3,4},{4,5},{5,6},{6,7},{8,9},{9,10},{10,11},{11... | collective-permute-start | bytes 208904 | tf_op jit(solution)/shard_map/ppermute | solution.py:405
  12.4 2.1 %collective-permute-start.3 = (f32[34,512]{1,0:T(8,128)S(1)}, f32[34,512]{1,0:T(8,128)S(1)}, u32[]{:S(2)}, u32[]{:S(2)}) collective-permute-start(f32[34,512]{1,0:T(8,128)S(1)} %pad_maximum_fusion.1), channel_id=1, source_target_pairs={{1,0},{2,1},{3,2},{4,3},{5,4},{6,5},{7,6},{9,8},{10,9},{11,10},{12... | collective-permute-start | bytes 208904 | tf_op jit(solution)/shard_map/ppermute | solution.py:406
  14.5 1.2 copy-done.3
  15.8 0.7 copy-done.12
  16.5 0.7 copy-done.13
  17.2 7.6 %ocean_pack.1 = f32[32,168,128]{2,1,0:T(8,128)S(1)} custom-call(s32[1,2048]{1,0:T(1,128)S(1)} %bitcast.47, s32[1,2048]{1,0:T(1,128)S(1)} %bitcast.48, f32[2048,128]{1,0:T(8,128)S(1)} %copy-done.3), custom_call_target="tpu_custom_call" | custom-call | flops 5368709120 | bytes 10000000 | tf_op jit(solution)/shard_map/ocean_pack/pallas_call | solution.py:382
  24.8 1.5 copy-done.1
  26.4 7.7 %all-to-all-start = ((f32[32,168,128]{2,1,0:T(8,128)}), f32[32,168,128]{2,1,0:T(8,128)S(1)}, u32[]{:S(2)}, u32[]{:S(2)}) async-start(f32[32,168,128]{2,1,0:T(8,128)} %copy-done.1), calls=%async_computation | async-start | bytes 5505024 | tf_op jit(solution)/shard_map/all_to_all | solution.py:411
  35.3 2.2 %copy-done = f32[32,64,512]{2,1,0:T(8,128)S(1)} copy-done((f32[32,64,512]{2,1,0:T(8,128)S(1)}, f32[32,64,512]{2,1,0:T(8,128)}, u32[]{:S(2)}) %copy-start) | copy-done | bytes 4194328
  37.5 6.2 %gather_tiles.1 = (f32[128,512]{1,0:T(8,128)S(1)}, f32[128,512]{1,0:T(8,128)S(1)}, f32[128,512]{1,0:T(8,128)S(1)}, f32[128,512]{1,0:T(8,128)S(1)}) custom-call(s32[4,512]{1,0:T(4,128)S(1)} %pad_add_fusion.index_ref, f32[2048,512]{1,0:T(8,128)S(1)} %bitcast.45, f32[208,512]{1,0:T(8,128)S(1)} %concatenate.14.rim_ref), custom_call_target="tpu_custom_call" | custom-call | tf_op jit(solution)/shard_map/gather_tiles/pallas_call | solution.py:450
  43.8 61.3 %contact_opening.1 = (f32[8,40,128]{2,1,0:T(8,128)S(1)}, f32[2,40,128]{2,1,0:T(8,128)S(1)}) custom-call(f32[128,512]{1,0:T(8,128)S(1)} %get-tuple-element.13.ox_ref, f32[128,512]{1,0:T(8,128)S(1)} %get-tuple-element.14.oy_ref, f32[128,512]{1,0:T(8,128)S(1)} %get-tuple-element.15.px_ref, f32[128,512]{1,0:T(8,128)S(1)} %get-tuple-element.16.py_ref, ...), custom_call_target="tpu_custom_call" | custom-call | flops 83886080 | bytes 100000000 | tf_op jit(solution)/shard_map/contact_opening/pallas_call | solution.py:475
  105.2 0.6 copy-done.14
  106.0 1.2 copy-done.2
  107.2 10.4 %ocean_force.1 = f32[8,2048]{1,0:T(8,128)S(1)} custom-call(s32[1,5120]{1,0:T(1,128)S(1)} %convert_element_type.21.index_ref, f32[32,168,128]{2,1,0:T(8,128)S(1)} %all-to-all-done.rows_ref, f32[2048,64]{1,0:T(8,128)S(1)} %bitcast.46), custom_call_target="tpu_custom_call" | custom-call | tf_op jit(solution)/shard_map/ocean_force/pallas_call | solution.py:528
  117.8 0.9 copy-done.9
  118.7 0.9 copy-done.11
  119.7 53.2 %contact_steps.1 = f32[4,40,128]{2,1,0:T(8,128)S(1)} custom-call(f32[128,512]{1,0:T(8,128)S(1)} %copy-done.5, f32[128,512]{1,0:T(8,128)S(1)} %copy-done.7, f32[128,512]{1,0:T(8,128)S(1)} %copy-done.9, f32[128,512]{1,0:T(8,128)S(1)} %copy-done.11, s32[8,512]{1,0:T(8,128)S(1)} %stack.5.meta_ref, f32[8,40,128]{2,1,0:T(8,128)S(1)} %get-tuple-element.17.state_ref, ...), custom_call_target="tpu_custom_call" | custom-call | flops 167772160 | bytes 100000000 | tf_op jit(solution)/shard_map/contact_steps/pallas_call | solution.py:475
  173.0 0.6 copy.25
  173.7 0.6 copy.24
  (68 shorter events, 1.1 us)
Async XLA Ops:
  1.6 7.0 %collective-permute-start.1 = (f32[64,512]{1,0:T(8,128)S(1)}, f32[64,512]{1,0:T(8,128)S(1)}, u32[]{:S(2)}, u32[]{:S(2)}) collective-permute-start(f32[64,512]{1,0:T(8,128)S(1)} %get-tuple-element.33), channel_id=1, source_target_pairs={{8,0},{16,8},{24,16},{9,1},{17,9},{25,17},{10,2},{18,10},{26,18},{... | collective-permute-start | bytes 393224 | tf_op jit(solution)/shard_map/ppermute | solution.py:401
  4.2 5.0 %collective-permute-start = (f32[64,512]{1,0:T(8,128)S(1)}, f32[64,512]{1,0:T(8,128)S(1)}, u32[]{:S(2)}, u32[]{:S(2)}) collective-permute-start(f32[64,512]{1,0:T(8,128)S(1)} %get-tuple-element.34), channel_id=1, source_target_pairs={{0,8},{8,16},{16,24},{1,9},{9,17},{17,25},{2,10},{10,18},{18,26},{... | collective-permute-start | bytes 393224 | tf_op jit(solution)/shard_map/ppermute | solution.py:400
  9.2 17.1 %collective-permute-start.2 = (f32[34,512]{1,0:T(8,128)S(1)}, f32[34,512]{1,0:T(8,128)S(1)}, u32[]{:S(2)}, u32[]{:S(2)}) collective-permute-start(f32[34,512]{1,0:T(8,128)S(1)} %pad_maximum_fusion), channel_id=1, source_target_pairs={{0,1},{1,2},{2,3},{3,4},{4,5},{5,6},{6,7},{8,9},{9,10},{10,11},{11... | collective-permute-start | bytes 208904 | tf_op jit(solution)/shard_map/ppermute | solution.py:405
  12.4 13.9 %collective-permute-start.3 = (f32[34,512]{1,0:T(8,128)S(1)}, f32[34,512]{1,0:T(8,128)S(1)}, u32[]{:S(2)}, u32[]{:S(2)}) collective-permute-start(f32[34,512]{1,0:T(8,128)S(1)} %pad_maximum_fusion.1), channel_id=1, source_target_pairs={{1,0},{2,1},{3,2},{4,3},{5,4},{6,5},{7,6},{9,8},{10,9},{11,10},{12... | collective-permute-start | bytes 208904 | tf_op jit(solution)/shard_map/ppermute | solution.py:406
  14.5 1.2 copy-start.3
  24.8 1.5 copy-start.1
  26.3 8.5 %copy-start.16 = (f32[32,64,2]{1,2,0:T(2,128)S(1)}, f32[32,64,2]{1,2,0:T(2,128)}, u32[]{:S(2)}) copy-start(f32[32,64,2]{1,2,0:T(2,128)} %param.14) | copy-start | bytes 49156
  26.3 8.5 %copy-start.17 = (f32[32,64,2]{1,2,0:T(2,128)S(1)}, f32[32,64,2]{1,2,0:T(2,128)}, u32[]{:S(2)}) copy-start(f32[32,64,2]{1,2,0:T(2,128)} %param.13) | copy-start | bytes 49156
  26.3 8.5 %copy-start.18 = (f32[32,64]{1,0:T(8,128)S(1)}, f32[32,64]{1,0:T(8,128)}, u32[]{:S(2)}) copy-start(f32[32,64]{1,0:T(8,128)} %param.15) | copy-start | bytes 24580
  26.3 8.7 %copy-start.19 = (s32[1,1,512,4]{2,3,1,0:T(4,128)S(1)}, s32[1,1,512,4]{2,3,1,0:T(4,128)}, u32[]{:S(2)}) copy-start(s32[1,1,512,4]{2,3,1,0:T(4,128)} %param.17) | copy-start | bytes 24580
  26.3 8.8 %copy-start.20 = (s32[8]{0:T(128)S(1)}, s32[8]{0:T(128)}, u32[]{:S(2)}) copy-start(s32[8]{0:T(128)} %constant.70.clone) | copy-start | bytes 100
  26.3 8.8 %copy-start.21 = (s32[8]{0:T(128)S(1)}, s32[8]{0:T(128)}, u32[]{:S(2)}) copy-start(s32[8]{0:T(128)} %constant.69.clone) | copy-start | bytes 100
  26.4 79.4 %all-to-all-start = ((f32[32,168,128]{2,1,0:T(8,128)}), f32[32,168,128]{2,1,0:T(8,128)S(1)}, u32[]{:S(2)}, u32[]{:S(2)}) async-start(f32[32,168,128]{2,1,0:T(8,128)} %copy-done.1), calls=%async_computation | async-start | bytes 5505024 | tf_op jit(solution)/shard_map/all_to_all | solution.py:411
  35.3 2.2 %copy-start = (f32[32,64,512]{2,1,0:T(8,128)S(1)}, f32[32,64,512]{2,1,0:T(8,128)}, u32[]{:S(2)}) copy-start(f32[32,64,512]{2,1,0:T(8,128)} %param.12) | copy-start | bytes 12582916
  43.7 61.4 %copy-start.4 = (f32[128,512]{1,0:T(8,128)}, f32[128,512]{1,0:T(8,128)S(1)}, u32[]{:S(2)}) copy-start(f32[128,512]{1,0:T(8,128)S(1)} %get-tuple-element.13.ox_ref) | copy-start | bytes 786436
  43.7 61.4 %copy-start.6 = (f32[128,512]{1,0:T(8,128)}, f32[128,512]{1,0:T(8,128)S(1)}, u32[]{:S(2)}) copy-start(f32[128,512]{1,0:T(8,128)S(1)} %get-tuple-element.14.oy_ref) | copy-start | bytes 786436
  43.8 61.4 %copy-start.8 = (f32[128,512]{1,0:T(8,128)}, f32[128,512]{1,0:T(8,128)S(1)}, u32[]{:S(2)}) copy-start(f32[128,512]{1,0:T(8,128)S(1)} %get-tuple-element.15.px_ref) | copy-start | bytes 786436
  43.8 61.4 %copy-start.10 = (f32[128,512]{1,0:T(8,128)}, f32[128,512]{1,0:T(8,128)S(1)}, u32[]{:S(2)}) copy-start(f32[128,512]{1,0:T(8,128)S(1)} %get-tuple-element.16.py_ref) | copy-start | bytes 786436
  105.8 12.0 %copy-start.5 = (f32[128,512]{1,0:T(8,128)S(1)}, f32[128,512]{1,0:T(8,128)}, u32[]{:S(2)}) copy-start(f32[128,512]{1,0:T(8,128)} %copy-done.4) | copy-start | bytes 786436
  105.8 12.0 %copy-start.7 = (f32[128,512]{1,0:T(8,128)S(1)}, f32[128,512]{1,0:T(8,128)}, u32[]{:S(2)}) copy-start(f32[128,512]{1,0:T(8,128)} %copy-done.6) | copy-start | bytes 786436
  105.8 12.0 %copy-start.15 = (f32[2,40,128]{2,1,0:T(8,128)S(1)}, f32[2,40,128]{2,1,0:T(8,128)}, u32[]{:S(2)}) copy-start(f32[2,40,128]{2,1,0:T(8,128)} %copy-done.14) | copy-start | bytes 122884
  105.9 1.2 copy-start.2
  117.8 1.0 copy-start.9
  118.7 0.9 copy-start.11
  (3 other events, 2.0 us)
